TPU v7x, 32 devices: a whole 2x2x4 slice. The times are simulated.
32 devices in a mesh: dp: 16 (over z, y, x), tensor: 2 (over core).
Axes of the slice: x: 2, y: 2, z: 4, core: 2. Of those that a mesh axis runs over, the one named last changes fastest.
Arguments:
- inputs: bfloat16 [16384, 1024], P('dp'), may hold values from -6 to 6
- segments: int32 [16, 1024], P('dp'), may hold values from 0 to 3, never falling along the last dimension, each value on 1 to 512 neighbouring positions
- mixer_gain: float32 [1024], replicated, may hold values from 0.5 to 1.5
- ssm_gate: bfloat16 [1024, 1536], P('dp', 'tensor'), may hold values from -0.1875 to 0.1875
- ssm_input: bfloat16 [1024, 1536], P('dp', 'tensor'), may hold values from -0.1875 to 0.1875
- step_weight: bfloat16 [1024, 24], P('dp', 'tensor'), may hold values from -0.09375 to 0.09375
- state_weight: bfloat16 [1024, 256], P('dp'), may hold values from -0.1875 to 0.1875
- conv_input: float32 [4, 1536], P(None, 'tensor'), may hold values from -3 to 3
- input_bias: float32 [1536], P('tensor'), may hold values from -3 to 3
- conv_state: float32 [4, 256], replicated, may hold values from -3 to 3
- state_bias: float32 [256], replicated, may hold values from -3 to 3
- step_bias: float32 [24], P('tensor'), may hold values from -5 to -1
- decay_log: float32 [24], P('tensor'), may hold values from 0 to 2.77
- skip_gain: float32 [24], P('tensor'), may hold values from 0.5 to 1.5
- ssm_norm: float32 [1536], P('tensor'), may hold values from 0.5 to 1.5
- ssm_output: bfloat16 [1536, 1024], P('tensor', 'dp'), may hold values from -0.15625 to 0.15625
- query_weight: bfloat16 [1024, 512], P('dp', 'tensor'), may hold values from -0.1875 to 0.1875
- key_matrix: bfloat16 [1024, 128], P('dp', 'tensor'), may hold values from -0.1875 to 0.1875
- value_matrix: bfloat16 [1024, 128], P('dp', 'tensor'), may hold values from -0.1875 to 0.1875
- output_weight: bfloat16 [512, 1024], P('tensor', 'dp'), may hold values from -2 to 2
- feed_gain: float32 [1024], replicated, may hold values from 0.5 to 1.5
- gate_weight: bfloat16 [1024, 2048], P('dp', 'tensor'), may hold values from -0.1875 to 0.1875
- up_weight: bfloat16 [1024, 2048], P('dp', 'tensor'), may hold values from -0.1875 to 0.1875
- down_weight: bfloat16 [2048, 1024], P('tensor', 'dp'), may hold values from -0.125 to 0.125
- upstream: bfloat16 [16384, 1024], P('dp'), may hold values from -6 to 6
Outputs:
- output: bfloat16 [16384, 1024], P('dp')
- grad_inputs: bfloat16 [16384, 1024], P('dp')
- grad_mixer_gain: float32 [1024], replicated
- grad_ssm_gate: float32 [1024, 1536], P('dp', 'tensor')
- grad_ssm_input: float32 [1024, 1536], P('dp', 'tensor')
- grad_step_weight: float32 [1024, 24], P('dp', 'tensor')
- grad_state_weight: float32 [1024, 256], P('dp')
- grad_conv_input: float32 [4, 1536], P(None, 'tensor')
- grad_input_bias: float32 [1536], P('tensor')
- grad_conv_state: float32 [4, 256], replicated
- grad_state_bias: float32 [256], replicated
- grad_step_bias: float32 [24], P('tensor')
- grad_decay_log: float32 [24], P('tensor')
- grad_skip_gain: float32 [24], P('tensor')
- grad_ssm_norm: float32 [1536], P('tensor')
- grad_ssm_output: float32 [1536, 1024], P('tensor', 'dp')
- grad_query_weight: float32 [1024, 512], P('dp', 'tensor')
- grad_key_weight: float32 [1024, 128], P('dp', 'tensor')
- grad_value_weight: float32 [1024, 128], P('dp', 'tensor')
- grad_output_weight: float32 [512, 1024], P('tensor', 'dp')
- grad_feed_gain: float32 [1024], replicated
- grad_gate_weight: float32 [1024, 2048], P('dp', 'tensor')
- grad_up_weight: float32 [1024, 2048], P('dp', 'tensor')
- grad_down_weight: float32 [2048, 1024], P('tensor', 'dp')
Inputs may be any that keep to these rules, and one draw needn't show every extreme that they name: `segments`: in each row the ids never fall, every id from 0 to 3 appears, each covers 1 to 512 positions and one covers exactly 512.
All inputs are finite; a program needn't handle non-finite values.
Results may differ from a plain program's by a relative error of at most 0.018.
Values may be sent and summed in bfloat16 or wider, within the bound.
A program may use at most 192 MiB of HBM per device.

v0:
```python
from functools import partial
import math

import jax
import jax.numpy as jnp
from jax import lax
from jax.sharding import PartitionSpec as P

HM = 24
HEAD_SIZE = 64
BLK = 128


epsilon = 1e-05
rope_base = 100000000000.0
masked_score = -1e30
highest_precision = lax.Precision.HIGHEST


def forward_dot(left, right):
    return jnp.dot(left, right, preferred_element_type=jnp.float32)


def back_dot(grad_rows, weights):
    return jnp.einsum("tj,ij->ti", grad_rows, weights, preferred_element_type=jnp.float32)


def outer_sum(left, right):
    return jnp.einsum("ti,tj->ij", left, right, preferred_element_type=jnp.float32)


def rms_scale(values):
    return lax.rsqrt(jnp.mean(values * values, axis=-1, keepdims=True) + epsilon)


def norm_back(values, score_scale, gain, grad_normed):
    scaled_grad = grad_normed * gain
    grad_values = score_scale * scaled_grad - values * score_scale**3 * jnp.mean(
        scaled_grad * values, axis=-1, keepdims=True
    )
    grad_gain = jnp.sum(grad_normed * values * score_scale, axis=0)
    return (grad_values, grad_gain)


def causal_conv(segment_ids, values, weights, biases):
    tap_count = weights.shape[0]
    summed = biases[None, :] + weights[tap_count - 1][None, :] * values
    for offset in range(1, tap_count):
        earlier = jnp.pad(values, ((offset, 0), (0, 0)))[:-offset]
        earlier_ids = jnp.pad(segment_ids, (offset, 0), constant_values=-1)[:-offset]
        summed = summed + weights[tap_count - 1 - offset][None, :] * jnp.where(
            (earlier_ids == segment_ids)[:, None], earlier, 0.0
        )
    return jax.nn.silu(summed)


def rope_tables(sequence_length, head_width):
    half_width = head_width // 2
    frequency = rope_base ** (-2.0 * jnp.arange(half_width, dtype=jnp.float32) / head_width)
    angles = jnp.arange(sequence_length, dtype=jnp.float32)[:, None] * frequency[None, :]
    return (jnp.cos(angles), jnp.sin(angles))


def turn(vectors, cosine_table, sine_table, direction):
    half_width = vectors.shape[-1] // 2
    shape_out = (vectors.shape[0],) + (1,) * (vectors.ndim - 2) + (half_width,)
    cos_part = cosine_table.reshape(shape_out)
    sin_part = direction * sine_table.reshape(shape_out)
    first_half = vectors[..., :half_width]
    second_half = vectors[..., half_width:]
    return jnp.concatenate(
        [
            first_half * cos_part - second_half * sin_part,
            second_half * cos_part + first_half * sin_part,
        ],
        axis=-1,
    )


def span_mix(heads_in, step_size, rate, state_in, state_out, segment_ids):
    sequence_length, head_count, head_width = heads_in.shape
    block_count = sequence_length // BLK
    states = state_in.shape[1]
    cumulative = jnp.cumsum(
        (-step_size * rate[None, :]).reshape(block_count, BLK, head_count), axis=1
    ).transpose(0, 2, 1)
    block_ids = segment_ids.reshape(block_count, BLK)
    scaled_in = (heads_in * step_size[:, :, None]).reshape(block_count, BLK, head_count, head_width)
    in_blocks = state_in.reshape(block_count, BLK, states)
    out_blocks = state_out.reshape(block_count, BLK, states)
    offsets = jnp.arange(BLK)
    allowed = (offsets[:, None] >= offsets[None, :])[None] & (
        block_ids[:, :, None] == block_ids[:, None, :]
    )
    spread = cumulative[:, :, :, None] - cumulative[:, :, None, :]
    decays = jnp.where(allowed[:, None], jnp.exp(jnp.where(allowed[:, None], spread, 0.0)), 0.0)
    intersection = jnp.einsum("ntk,nsk->nts", out_blocks, in_blocks, precision=highest_precision)
    inside = jnp.einsum(
        "nhts,nshp->nthp", decays * intersection[:, None], scaled_in, precision=highest_precision
    )
    last_ids = block_ids[:, -1]
    to_end = jnp.where(
        (block_ids == last_ids[:, None])[:, None, :],
        jnp.exp(cumulative[:, :, -1:] - cumulative),
        0.0,
    )
    local_state = jnp.einsum(
        "nhs,nshp,nsk->nhpk", to_end, scaled_in, in_blocks, precision=highest_precision
    )
    carried = jnp.concatenate([jnp.zeros((1,), dtype=bool), last_ids[1:] == last_ids[:-1]])

    def advance(running, pieces):
        fresh_state, factor, keep_going = pieces
        return (jnp.where(keep_going, factor[:, None, None] * running, 0.0) + fresh_state, running)

    start_state = jnp.zeros(local_state.shape[1:], local_state.dtype)
    _, entering = lax.scan(
        advance, start_state, (local_state, jnp.exp(cumulative[:, :, -1]), carried)
    )
    earlier_ids = jnp.concatenate([jnp.full((1,), -1, jnp.int32), last_ids[:-1]])
    from_start = jnp.where(
        (block_ids == earlier_ids[:, None])[:, None, :], jnp.exp(cumulative), 0.0
    )
    across = (
        jnp.einsum("ntk,nhpk->nthp", out_blocks, entering, precision=highest_precision)
        * from_start.transpose(0, 2, 1)[:, :, :, None]
    )
    return (inside + across).reshape(sequence_length, head_count, head_width)


def ssm_core(
    segment_ids,
    inner_raw,
    state_conv,
    step_raw,
    gate_z,
    conv_input,
    input_bias,
    step_bias,
    decay_log,
    skip_gain,
):
    sequence_length = inner_raw.shape[0]
    head_count = step_raw.shape[1]
    inner_conv = causal_conv(segment_ids, inner_raw, conv_input, input_bias)
    step_size = jax.nn.softplus(step_raw + step_bias)
    heads_in = inner_conv.reshape(sequence_length, head_count, -1)
    states = state_conv.shape[1] // 2
    ssm_mixed = span_mix(
        heads_in,
        step_size,
        jnp.exp(decay_log),
        state_conv[:, :states],
        state_conv[:, states:],
        segment_ids,
    )
    ssm_mixed = ssm_mixed + skip_gain[None, :, None] * heads_in
    return ssm_mixed.reshape(sequence_length, -1) * jax.nn.silu(gate_z)


def block_scores(query_rows, projected_keys, segment_ids, first_row, score_scale):
    row_count = query_rows.shape[0]
    raw_scores = (
        jnp.einsum("havb,oab->avho", query_rows, projected_keys, preferred_element_type=jnp.float32)
        * score_scale
    )
    query_pos = first_row + jnp.arange(row_count)
    key_pos = jnp.arange(segment_ids.shape[0])
    query_ids = lax.dynamic_slice_in_dim(segment_ids, first_row, row_count)
    allowed = (query_pos[:, None] >= key_pos[None, :]) & (
        query_ids[:, None] == segment_ids[None, :]
    )
    return jnp.where(allowed, raw_scores, masked_score)


def on_device(
    inputs,
    segments,
    mixer_gain,
    ssm_gate,
    ssm_input,
    step_weight,
    state_weight,
    conv_input,
    input_bias,
    conv_state,
    state_bias,
    step_bias,
    decay_log,
    skip_gain,
    ssm_norm,
    ssm_output,
    query_weight,
    key_matrix,
    value_matrix,
    output_weight,
    feed_gain,
    gate_weight,
    up_weight,
    down_weight,
    upstream,
):
    segment_ids = segments.reshape(-1)
    sequence_length = inputs.shape[0]
    gathered = (
        lax.all_gather(ssm_gate, "dp", axis=0, tiled=True),
        lax.all_gather(ssm_input, "dp", axis=0, tiled=True),
        lax.all_gather(step_weight, "dp", axis=0, tiled=True),
        lax.all_gather(state_weight, "dp", axis=0, tiled=True),
        lax.all_gather(query_weight, "dp", axis=0, tiled=True),
        lax.all_gather(key_matrix, "dp", axis=0, tiled=True),
        lax.all_gather(value_matrix, "dp", axis=0, tiled=True),
        lax.all_gather(ssm_output, "dp", axis=1, tiled=True),
        lax.all_gather(output_weight, "dp", axis=1, tiled=True),
        lax.all_gather(gate_weight, "dp", axis=0, tiled=True),
        lax.all_gather(up_weight, "dp", axis=0, tiled=True),
        lax.all_gather(down_weight, "dp", axis=1, tiled=True),
    )
    (
        full_gate,
        full_input,
        full_step,
        full_state,
        full_query,
        full_key,
        full_value,
        full_ssm_out,
        full_output,
        full_feed_gate,
        full_feed_up,
        full_down,
    ) = gathered
    tokens = inputs.astype(jnp.float32)
    first_scale = rms_scale(tokens)
    hidden_activations = (tokens * first_scale * mixer_gain).astype(jnp.bfloat16)
    gate_z = forward_dot(hidden_activations, full_gate)
    inner_raw = forward_dot(hidden_activations, full_input)
    step_raw = forward_dot(hidden_activations, full_step)
    state_raw = forward_dot(hidden_activations, full_state)
    query_raw = forward_dot(hidden_activations, full_query)
    key_raw = forward_dot(hidden_activations, full_key)
    value_raw = forward_dot(hidden_activations, full_value)
    state_conv, state_pull = jax.vjp(
        partial(causal_conv, segment_ids), state_raw, conv_state, state_bias
    )
    gated_ssm, ssm_pull = jax.vjp(
        partial(ssm_core, segment_ids),
        inner_raw,
        state_conv,
        step_raw,
        gate_z,
        conv_input,
        input_bias,
        step_bias,
        decay_log,
        skip_gain,
    )
    all_squares = lax.psum(jnp.sum(gated_ssm * gated_ssm, axis=-1, keepdims=True), "tensor")
    ssm_scale = lax.rsqrt(all_squares / (HM * HEAD_SIZE) + epsilon)
    normed = (gated_ssm * ssm_scale * ssm_norm).astype(jnp.bfloat16)
    local_kv = key_raw.shape[1] // HEAD_SIZE
    group_size = query_raw.shape[1] // HEAD_SIZE // local_kv
    score_scale = 1.0 / math.sqrt(HEAD_SIZE)
    cosine_table, sine_table = rope_tables(sequence_length, HEAD_SIZE)
    query_rows = turn(
        query_raw.reshape(sequence_length, local_kv, group_size, HEAD_SIZE),
        cosine_table,
        sine_table,
        1.0,
    ).astype(jnp.bfloat16)
    projected_keys = turn(
        key_raw.reshape(sequence_length, local_kv, HEAD_SIZE), cosine_table, sine_table, 1.0
    ).astype(jnp.bfloat16)
    projected_values = value_raw.reshape(sequence_length, local_kv, HEAD_SIZE).astype(jnp.bfloat16)
    block_rows = min(512, sequence_length)
    attended_parts = []
    log_totals = []
    for first_row in range(0, sequence_length, block_rows):
        attention_scores = block_scores(
            query_rows[first_row : first_row + block_rows],
            projected_keys,
            segment_ids,
            first_row,
            score_scale,
        )
        row_max = jnp.max(attention_scores, axis=-1, keepdims=True)
        exponent = jnp.exp(attention_scores - row_max)
        row_total = jnp.sum(exponent, axis=-1, keepdims=True)
        attention_lowered = (exponent / row_total).astype(jnp.bfloat16)
        attended_parts.append(
            jnp.einsum(
                "woyu,uwq->ywoq",
                attention_lowered,
                projected_values,
                preferred_element_type=jnp.float32,
            )
        )
        log_totals.append(row_max + jnp.log(row_total))
    attention_result = (
        jnp.concatenate(attended_parts, axis=0).reshape(sequence_length, -1).astype(jnp.bfloat16)
    )
    mixer_part = forward_dot(normed, full_ssm_out) + forward_dot(attention_result, full_output)
    middle = tokens + lax.psum(mixer_part.astype(jnp.bfloat16), "tensor").astype(jnp.float32)
    second_scale = rms_scale(middle)
    hidden_two = (middle * second_scale * feed_gain).astype(jnp.bfloat16)
    gate_value = forward_dot(hidden_two, full_feed_gate)
    up_value = forward_dot(hidden_two, full_feed_up)
    product = (jax.nn.silu(gate_value) * up_value).astype(jnp.bfloat16)
    feed_out = lax.psum(forward_dot(product, full_down).astype(jnp.bfloat16), "tensor").astype(
        jnp.float32
    )
    output = (middle + feed_out).astype(jnp.bfloat16)
    regathered = (
        lax.all_gather(ssm_gate, "dp", axis=0, tiled=True),
        lax.all_gather(ssm_input, "dp", axis=0, tiled=True),
        lax.all_gather(step_weight, "dp", axis=0, tiled=True),
        lax.all_gather(state_weight, "dp", axis=0, tiled=True),
        lax.all_gather(query_weight, "dp", axis=0, tiled=True),
        lax.all_gather(key_matrix, "dp", axis=0, tiled=True),
        lax.all_gather(value_matrix, "dp", axis=0, tiled=True),
        lax.all_gather(ssm_output, "dp", axis=1, tiled=True),
        lax.all_gather(output_weight, "dp", axis=1, tiled=True),
        lax.all_gather(gate_weight, "dp", axis=0, tiled=True),
        lax.all_gather(up_weight, "dp", axis=0, tiled=True),
        lax.all_gather(down_weight, "dp", axis=1, tiled=True),
    )
    (
        back_gate,
        back_input,
        back_step,
        back_state,
        back_query,
        back_key,
        back_value,
        back_ssm_out,
        back_output,
        back_feed_gate,
        back_feed_up,
        back_down,
    ) = regathered
    grad_down_weight = outer_sum(product, upstream)
    grad_product = back_dot(upstream, back_down)
    gate_sigmoid = jax.nn.sigmoid(gate_value)
    grad_gate = (
        grad_product * up_value * gate_sigmoid * (1.0 + gate_value * (1.0 - gate_sigmoid))
    ).astype(jnp.bfloat16)
    grad_up = (grad_product * jax.nn.silu(gate_value)).astype(jnp.bfloat16)
    grad_gate_weight = outer_sum(hidden_two, grad_gate)
    grad_up_weight = outer_sum(hidden_two, grad_up)
    feed_shards = (grad_gate_weight, grad_up_weight, grad_down_weight)
    grad_hidden_two = lax.psum(
        (back_dot(grad_gate, back_feed_gate) + back_dot(grad_up, back_feed_up)).astype(
            jnp.bfloat16
        ),
        "tensor",
    ).astype(jnp.float32)
    grad_mid_norm, grad_feed_gain = norm_back(middle, second_scale, feed_gain, grad_hidden_two)
    grad_middle = upstream.astype(jnp.float32) + grad_mid_norm
    grad_branch = grad_middle.astype(jnp.bfloat16)
    grad_ssm_output = outer_sum(normed, grad_branch)
    grad_output_weight = outer_sum(attention_result, grad_branch)
    grad_normed = back_dot(grad_branch, back_ssm_out)
    grad_attended = (
        back_dot(grad_branch, back_output)
        .astype(jnp.bfloat16)
        .reshape(sequence_length, local_kv, group_size, HEAD_SIZE)
    )
    scaled_grad = grad_normed * ssm_norm
    grad_ssm_norm = jnp.sum(grad_normed * gated_ssm * ssm_scale, axis=0)
    cross_sum = lax.psum(jnp.sum(scaled_grad * gated_ssm, axis=-1, keepdims=True), "tensor")
    grad_gated = ssm_scale * scaled_grad - gated_ssm * ssm_scale**3 * cross_sum / (HM * HEAD_SIZE)
    (
        grad_inner,
        grad_state_conv,
        grad_step_raw,
        grad_gate_z,
        grad_conv_input,
        grad_input_bias,
        grad_step_bias,
        grad_decay_log,
        grad_skip_gain,
    ) = ssm_pull(grad_gated)
    grad_query_parts = []
    grad_key_sum = jnp.zeros((sequence_length, local_kv, HEAD_SIZE), jnp.float32)
    grad_value_sum = jnp.zeros((sequence_length, local_kv, HEAD_SIZE), jnp.float32)
    for block_index, first_row in enumerate(range(0, sequence_length, block_rows)):
        query_tile_rows = query_rows[first_row : first_row + block_rows]
        block_gradient = grad_attended[first_row : first_row + block_rows]
        attention_scores = block_scores(
            query_tile_rows, projected_keys, segment_ids, first_row, score_scale
        )
        attention_weights = jnp.exp(attention_scores - log_totals[block_index])
        grad_probs = jnp.einsum(
            "havb,oab->avho", block_gradient, projected_values, preferred_element_type=jnp.float32
        )
        inner_term = jnp.sum(grad_probs * attention_weights, axis=-1, keepdims=True)
        score_gradient = (attention_weights * (grad_probs - inner_term)).astype(jnp.bfloat16)
        grad_query_parts.append(
            jnp.einsum(
                "woyu,uwq->ywoq", score_gradient, projected_keys, preferred_element_type=jnp.float32
            )
            * score_scale
        )
        grad_key_sum = (
            grad_key_sum
            + jnp.einsum(
                "mhvu,vmhi->umi",
                score_gradient,
                query_tile_rows,
                preferred_element_type=jnp.float32,
            )
            * score_scale
        )
        grad_value_sum = grad_value_sum + jnp.einsum(
            "mhvu,vmhi->umi",
            attention_weights.astype(jnp.bfloat16),
            block_gradient,
            preferred_element_type=jnp.float32,
        )
    grad_query = (
        turn(jnp.concatenate(grad_query_parts, axis=0), cosine_table, sine_table, -1.0)
        .reshape(sequence_length, -1)
        .astype(jnp.bfloat16)
    )
    grad_key = (
        turn(grad_key_sum, cosine_table, sine_table, -1.0)
        .reshape(sequence_length, -1)
        .astype(jnp.bfloat16)
    )
    grad_value = grad_value_sum.reshape(sequence_length, -1).astype(jnp.bfloat16)
    grad_z_low = grad_gate_z.astype(jnp.bfloat16)
    grad_inner_low = grad_inner.astype(jnp.bfloat16)
    grad_step_low = grad_step_raw.astype(jnp.bfloat16)
    grad_ssm_gate = outer_sum(hidden_activations, grad_z_low)
    grad_ssm_input = outer_sum(hidden_activations, grad_inner_low)
    grad_step_weight = outer_sum(hidden_activations, grad_step_low)
    grad_query_weight = outer_sum(hidden_activations, grad_query)
    grad_key_weight = outer_sum(hidden_activations, grad_key)
    grad_value_weight = outer_sum(hidden_activations, grad_value)
    partial_hidden = (
        back_dot(grad_z_low, back_gate)
        + back_dot(grad_inner_low, back_input)
        + back_dot(grad_step_low, back_step)
        + back_dot(grad_query, back_query)
        + back_dot(grad_key, back_key)
        + back_dot(grad_value, back_value)
    )
    hidden_sum, state_sum = (
        lax.psum(partial_hidden.astype(jnp.bfloat16), "tensor").astype(jnp.float32),
        lax.psum(grad_state_conv.astype(jnp.bfloat16), "tensor").astype(jnp.float32),
    )
    grad_state_raw, grad_conv_state, grad_state_bias = state_pull(state_sum)
    grad_state_low = grad_state_raw.astype(jnp.bfloat16)
    grad_state_weight = outer_sum(hidden_activations, grad_state_low)
    grad_hidden = hidden_sum + back_dot(grad_state_low, back_state)
    grad_in_norm, grad_mixer_gain = norm_back(tokens, first_scale, mixer_gain, grad_hidden)
    grad_inputs = (grad_middle + grad_in_norm).astype(jnp.bfloat16)
    weight_shards = (
        lax.psum_scatter(grad_ssm_gate, "dp", scatter_dimension=0, tiled=True),
        lax.psum_scatter(grad_ssm_input, "dp", scatter_dimension=0, tiled=True),
        lax.psum_scatter(grad_step_weight, "dp", scatter_dimension=0, tiled=True),
        lax.psum_scatter(grad_state_weight, "dp", scatter_dimension=0, tiled=True),
        lax.psum_scatter(grad_ssm_output, "dp", scatter_dimension=1, tiled=True),
        lax.psum_scatter(grad_query_weight, "dp", scatter_dimension=0, tiled=True),
        lax.psum_scatter(grad_key_weight, "dp", scatter_dimension=0, tiled=True),
        lax.psum_scatter(grad_value_weight, "dp", scatter_dimension=0, tiled=True),
        lax.psum_scatter(grad_output_weight, "dp", scatter_dimension=1, tiled=True),
        lax.psum_scatter(feed_shards[0], "dp", scatter_dimension=0, tiled=True),
        lax.psum_scatter(feed_shards[1], "dp", scatter_dimension=0, tiled=True),
        lax.psum_scatter(feed_shards[2], "dp", scatter_dimension=1, tiled=True),
    )
    small_sums = lax.psum(
        (
            grad_mixer_gain,
            grad_conv_input,
            grad_input_bias,
            grad_conv_state,
            grad_state_bias,
            grad_step_bias,
            grad_decay_log,
            grad_skip_gain,
            grad_ssm_norm,
            grad_feed_gain,
        ),
        "dp",
    )
    return (
        output,
        grad_inputs,
        small_sums[0],
        weight_shards[0],
        weight_shards[1],
        weight_shards[2],
        weight_shards[3],
        small_sums[1],
        small_sums[2],
        small_sums[3],
        small_sums[4],
        small_sums[5],
        small_sums[6],
        small_sums[7],
        small_sums[8],
        weight_shards[4],
        weight_shards[5],
        weight_shards[6],
        weight_shards[7],
        weight_shards[8],
        small_sums[9],
        weight_shards[9],
        weight_shards[10],
        weight_shards[11],
    )


def solution(mesh):
    return jax.shard_map(
        on_device,
        mesh=mesh,
        in_specs=(
            P("dp", None),
            P("dp", None),
            P(),
            P("dp", "tensor"),
            P("dp", "tensor"),
            P("dp", "tensor"),
            P("dp", None),
            P(None, "tensor"),
            P("tensor"),
            P(),
            P(),
            P("tensor"),
            P("tensor"),
            P("tensor"),
            P("tensor"),
            P("tensor", "dp"),
            P("dp", "tensor"),
            P("dp", "tensor"),
            P("dp", "tensor"),
            P("tensor", "dp"),
            P(),
            P("dp", "tensor"),
            P("dp", "tensor"),
            P("tensor", "dp"),
            P("dp", None),
        ),
        out_specs=(
            P("dp", None),
            P("dp", None),
            P(),
            P("dp", "tensor"),
            P("dp", "tensor"),
            P("dp", "tensor"),
            P("dp", None),
            P(None, "tensor"),
            P("tensor"),
            P(),
            P(),
            P("tensor"),
            P("tensor"),
            P("tensor"),
            P("tensor"),
            P("tensor", "dp"),
            P("dp", "tensor"),
            P("dp", "tensor"),
            P("dp", "tensor"),
            P("tensor", "dp"),
            P(),
            P("dp", "tensor"),
            P("dp", "tensor"),
            P("tensor", "dp"),
        ),
        check_vma=False,
    )
```

profile of v0, /device:TPU:0, one launch (start us, length us, event | category | flops | bytes accessed | tf_op | source)
XLA Modules:
  0.0 2121.7 jit_solution(4857133008984561617)
XLA Ops:
  18.3 43.3 %all-gather = bf16[16,64,12]{1,2,0:T(8,128)(2,1)S(1)} all-gather(bf16[1,64,12]{1,2,0:T(8,128)(2,1)} %bitcast.501), channel_id=1, replica_groups=mesh['dp'=16,'tensor'=2] {'dp'}, dimensions={0}, use_global_device_ids=true | all-gather | bytes 26112 | tf_op jit(solution)/shard_map/all_gather | solution.py:208
  65.5 23.3 %fusion.219 = f32[8,128,12]{2,0,1:T(8,128)S(1)} fusion(f32[8,128,12]{2,0,1:T(8,128)S(1)} %copy.237), kind=kOutput, calls=%fused_computation.355 | output fusion | flops 1560576 | bytes 98304 | tf_op jit(solution)/shard_map/jvp(jit(cumsum))/reduce_window_sum | solution.py:84
  99.7 37.8 %all_gather.54 = bf16[1024,64]{1,0:T(8,128)(2,1)S(1)} all-gather(bf16[64,64]{1,0:T(8,128)(2,1)} %param.46), channel_id=1, replica_groups=mesh['dp'=16,'tensor'=2] {'dp'}, dimensions={0}, use_global_device_ids=true | all-gather | bytes 139264 | tf_op jit(solution)/shard_map/all_gather | solution.py:211
  137.5 39.8 %all_gather.53 = bf16[1024,64]{1,0:T(8,128)(2,1)S(1)} all-gather(bf16[64,64]{1,0:T(8,128)(2,1)} %param.47), channel_id=1, replica_groups=mesh['dp'=16,'tensor'=2] {'dp'}, dimensions={0}, use_global_device_ids=true | all-gather | bytes 139264 | tf_op jit(solution)/shard_map/all_gather | solution.py:212
  179.2 41.8 %all_gather.50 = bf16[1024,256]{1,0:T(8,128)(2,1)} all-gather(bf16[64,256]{1,0:T(8,128)(2,1)} %param.35), channel_id=1, replica_groups=mesh['dp'=16,'tensor'=2] {'dp'}, dimensions={0}, use_global_device_ids=true | all-gather | bytes 557056 | tf_op jit(solution)/shard_map/all_gather | solution.py:209
  221.1 40.7 %all_gather.55 = bf16[1024,256]{1,0:T(8,128)(2,1)S(1)} all-gather(bf16[64,256]{1,0:T(8,128)(2,1)} %param.45), channel_id=1, replica_groups=mesh['dp'=16,'tensor'=2] {'dp'}, dimensions={0}, use_global_device_ids=true | all-gather | bytes 557056 | tf_op jit(solution)/shard_map/all_gather | solution.py:210
  261.8 41.1 %all_gather.56 = bf16[256,1024]{0,1:T(8,128)(2,1)} all-gather(bf16[256,64]{0,1:T(8,128)(2,1)} %param.48), channel_id=1, replica_groups=mesh['dp'=16,'tensor'=2] {'dp'}, dimensions={1}, use_global_device_ids=true | all-gather | bytes 557056 | tf_op jit(solution)/shard_map/all_gather | solution.py:214
  337.9 17.3 fusion.75
  368.3 40.3 %while.35 = (s32[]{:T(128)}, f32[12,64,128]{2,1,0:T(8,128)S(1)}, f32[8,12,64,128]{3,2,1,0:T(8,128)}, f32[8,12,1,1]{1,3,2,0:T(1,128)}, pred[8]{0:T(512)(128)(4,1)...) while((s32[]{:T(128)}, f32[12,64,128]{2,1,0:T(8,128)S(1)}, ...), condition=%wide.region_3.4_spmd.clone, body=%wide.region_2.3_spmd.clone.sunk | while | flops 491523 | bytes 1967383 | solution.py:117
  408.7 5.0 fusion.223
  413.7 13.0 bitcast_add_fusion.3
  435.3 7.0 multiply_reduce_fusion.11
  454.0 16.8 all-reduce.33.cloned.1.call-done
  475.4 60.3 %all-gather.16.cloned.1.call-done = bf16[1024,1024]{1,0:T(8,128)(2,1)} async-done(((bf16[64,1024]{1,0:T(8,128)(2,1)}), bf16[1024,1024]{1,0:T(8,128)(2,1)}) %all-gather.16.cloned.1.call-update) | async-done | bytes 2097168 | tf_op jit(solution)/shard_map/all_gather | solution.py:216
  535.7 6.6 fusion.226
  542.3 55.8 %all-gather.14.cloned.1.call-done = bf16[1024,1024]{1,0:T(8,128)(2,1)} async-done(((bf16[64,1024]{1,0:T(8,128)(2,1)}), bf16[1024,1024]{1,0:T(8,128)(2,1)}) %all-gather.14.cloned.1.call-update) | async-done | bytes 2097168 | tf_op jit(solution)/shard_map/all_gather | solution.py:215
  598.1 6.6 fusion.225
  604.7 56.0 %all-gather.18.cloned.1.call-done = bf16[1024,1024]{0,1:T(8,128)(2,1)} async-done(((bf16[1024,64]{0,1:T(8,128)(2,1)}), bf16[1024,1024]{0,1:T(8,128)(2,1)}) %all-gather.18.cloned.1.call-update) | async-done | bytes 2097168 | tf_op jit(solution)/shard_map/all_gather | solution.py:217
  660.7 9.9 multiply_convert_fusion
  683.5 6.2 convolution_convert_fusion
  689.7 8.1 all-reduce.35.cloned.1.call-done
  714.6 8.5 multiply_reduce_fusion.4
  731.8 6.2 fusion.104
  745.3 51.6 %while.36 = (s32[]{:T(128)}, f32[12,64,128]{2,1,0:T(8,128)S(1)}, f32[8,12,64,128]{3,2,1,0:T(8,128)}, f32[8,12]{1,0:T(8,128)}, f32[8,12,64,128]{3,2,1,0:T(8,128)}...) while((s32[]{:T(128)}, f32[12,64,128]{2,1,0:T(8,128)S(1)}, ...), condition=%wide.region_19.20_spmd.clone, body=%wide.region_17.19_spmd.clone.sunk | while | flops 688120 | bytes 2359747 | solution.py:117
  797.0 9.3 fusion.105
  806.4 5.5 multiply_reduce_fusion.2
  839.8 17.1 fusion.52
  868.1 7.4 bitcast_add_fusion.2
  890.1 6.7 fusion.33
  935.7 6.8 fusion.240
  943.0 6.9 fusion.238
  950.0 7.2 fusion.239
  957.8 6.2 fusion.204
  969.0 5.0 fusion.233
  981.7 52.1 %reduce-scatter.37.cloned.1.call-done = f32[64,12]{1,0:T(8,128)} async-done(((f32[1024,12]{1,0:T(8,128)}), f32[64,12]{1,0:T(8,128)}) %reduce-scatter.37.cloned.1.call-update) | async-done | bytes 3088
  1035.4 5.8 fusion.43
  1041.2 72.9 %all-reduce.27 = (f32[1024]{0:T(1024)}, f32[4,768]{1,0:T(4,128)}, f32[768]{0:T(1024)}, f32[4,256]{1,0:T(4,128)}, f32[256]{0:T(256)}, /*index=5*/f32[12]{0:T(128)...) all-reduce(f32[1024]{0:T(1024)S(1)} %get-tuple-element.315, ...), channel_id=1, replica_groups=mesh['dp'=16,'tensor'=2] {'dp'}, use_global_device_ids=true, to_apply=%region_33.34 | all-reduce | flops 7972 | bytes 63776 | tf_op jit(solution)/shard_map/psum | solution.py:472
  1114.1 7.5 fusion.40
  1121.6 63.8 %reduce-scatter.25.cloned.1.call-done = f32[64,64]{1,0:T(8,128)} async-done(((f32[1024,64]{1,0:T(8,128)}), f32[64,64]{1,0:T(8,128)}) %reduce-scatter.25.cloned.1.call-update) | async-done | bytes 16400 | tf_op jit(solution)/shard_map/reduce_scatter | solution.py:465
  1185.4 76.8 %reduce-scatter.29.cloned.1.call-done = f32[256,64]{0,1:T(8,128)} async-done(((f32[256,1024]{0,1:T(8,128)}), f32[256,64]{0,1:T(8,128)}) %reduce-scatter.29.cloned.1.call-update) | async-done | bytes 65552 | tf_op jit(solution)/shard_map/reduce_scatter | solution.py:467
  1262.2 77.0 %reduce-scatter.23.cloned.1.call-done = f32[64,256]{1,0:T(8,128)} async-done(((f32[1024,256]{1,0:T(8,128)}), f32[64,256]{1,0:T(8,128)}) %reduce-scatter.23.cloned.1.call-update) | async-done | bytes 65552 | tf_op jit(solution)/shard_map/reduce_scatter | solution.py:464
  1339.2 94.2 %reduce-scatter.35.cloned.1.call-done = f32[1024,64]{0,1:T(8,128)} async-done(((f32[1024,1024]{0,1:T(8,128)}), f32[1024,64]{0,1:T(8,128)}) %reduce-scatter.35.cloned.1.call-update) | async-done | bytes 262160 | tf_op jit(solution)/shard_map/reduce_scatter | solution.py:470
  1433.4 97.5 %reduce-scatter.31.cloned.1.call-done = f32[64,1024]{1,0:T(8,128)} async-done(((f32[1024,1024]{1,0:T(8,128)}), f32[64,1024]{1,0:T(8,128)}) %reduce-scatter.31.cloned.1.call-update) | async-done | bytes 262160 | tf_op jit(solution)/shard_map/reduce_scatter | solution.py:468
  1530.9 97.5 %reduce-scatter.33.cloned.1.call-done = f32[64,1024]{1,0:T(8,128)} async-done(((f32[1024,1024]{1,0:T(8,128)}), f32[64,1024]{1,0:T(8,128)}) %reduce-scatter.33.cloned.1.call-update) | async-done | bytes 262160 | tf_op jit(solution)/shard_map/reduce_scatter | solution.py:469
  1628.3 135.7 %reduce-scatter.21.cloned.1.call-done = f32[768,64]{0,1:T(8,128)} async-done(((f32[768,1024]{0,1:T(8,128)}), f32[768,64]{0,1:T(8,128)}) %reduce-scatter.21.cloned.1.call-update) | async-done | bytes 196624 | tf_op jit(solution)/shard_map/reduce_scatter | solution.py:463
  1764.1 135.6 %reduce-scatter.15.cloned.1.call-done = f32[64,768]{1,0:T(8,128)} async-done(((f32[1024,768]{1,0:T(8,128)}), f32[64,768]{1,0:T(8,128)}) %reduce-scatter.15.cloned.1.call-update) | async-done | bytes 196624 | tf_op jit(solution)/shard_map/reduce_scatter | solution.py:459
  1899.7 135.2 %reduce-scatter.17.cloned.1.call-done = f32[64,768]{1,0:T(8,128)} async-done(((f32[1024,768]{1,0:T(8,128)}), f32[64,768]{1,0:T(8,128)}) %reduce-scatter.17.cloned.1.call-update) | async-done | bytes 196624 | tf_op jit(solution)/shard_map/reduce_scatter | solution.py:460
  2034.9 79.8 %reduce-scatter.19.cloned.1.call-done = f32[64,256]{1,0:T(8,128)} async-done(((f32[1024,256]{1,0:T(8,128)}), f32[64,256]{1,0:T(8,128)}) %reduce-scatter.19.cloned.1.call-update) | async-done | bytes 65552 | tf_op jit(solution)/shard_map/reduce_scatter | solution.py:462
  (657 shorter events, 344.0 us)
Async XLA Ops:
  7.2 327.4 %all-gather.8.cloned.1.call-start = ((), (), s32[]{:S(2)}) async-start(), calls=%async_computation.12 | async-start | bytes 1671168 | tf_op jit(solution)/shard_map/all_gather | solution.py:207
  7.9 427.4 %all-gather.10.cloned.1.call-start = ((), (), s32[]{:S(2)}) async-start(), calls=%async_computation.13 | async-start | bytes 1671168 | tf_op jit(solution)/shard_map/all_gather | solution.py:206
  8.7 436.7 %all-gather.12.cloned.1.call-start = ((), (), s32[]{:S(2)}) async-start(), calls=%async_computation.14 | async-start | bytes 1671168 | tf_op jit(solution)/shard_map/all_gather | solution.py:213
  9.4 461.4 %all-reduce.33.cloned.1.call-start = ((), (), s32[]{:S(2)}) async-start(), calls=%async_computation.15 | async-start | bytes 4194304 | tf_op jit(solution)/shard_map/psum | solution.py:303
  15.6 48.3 %copy-start.169 = (f32[12]{0:T(128)}, f32[12]{0:T(128)S(1)}, u32[]{:S(2)}) copy-start(f32[12]{0:T(128)S(1)} %exp.57) | copy-start | bytes 148
  15.6 48.3 %copy-start.173 = (f32[12]{0:T(128)S(1)}, f32[12]{0:T(128)}, u32[]{:S(2)}) copy-start(f32[12]{0:T(128)} %param.40) | copy-start | bytes 148
  18.3 43.4 %copy-start.121 = (f32[1024]{0:T(1024)}, f32[1024]{0:T(1024)S(1)}, u32[]{:S(2)}) copy-start(f32[1024]{0:T(1024)S(1)} %get-tuple-element.416) | copy-start | bytes 12292
  63.9 371.5 %copy-start = (bf16[1024,1024]{1,0:T(8,128)(2,1)}, bf16[1024,1024]{1,0:T(8,128)(2,1)S(1)}, u32[]{:S(2)}) copy-start(bf16[1024,1024]{1,0:T(8,128)(2,1)S(1)} %fusion.36) | copy-start | bytes 6291460
  88.9 221.9 %copy-start.17 = (f32[8,128,12]{2,0,1:T(8,128)}, f32[8,128,12]{2,0,1:T(8,128)S(1)}, u32[]{:S(2)}) copy-start(f32[8,128,12]{2,0,1:T(8,128)S(1)} %fusion.219) | copy-start | bytes 147460
  88.9 221.9 %copy-start.100 = (f32[8,12]{1,0:T(8,128)}, f32[8,12]{1,0:T(8,128)S(1)}, u32[]{:S(2)}) copy-start(f32[8,12]{1,0:T(8,128)S(1)} %slice_bitcast_fusion.2) | copy-start | bytes 1156
  91.6 246.2 %copy-start.105 = (pred[1024]{0:T(1024)(128)(4,1)}, pred[1024]{0:T(1024)(128)(4,1)S(1)}, u32[]{:S(2)}) copy-start(pred[1024]{0:T(1024)(128)(4,1)S(1)} %get-tuple-element.429) | copy-start | bytes 3076
  91.6 246.2 %copy-start.107 = (pred[1024]{0:T(1024)(128)(4,1)}, pred[1024]{0:T(1024)(128)(4,1)S(1)}, u32[]{:S(2)}) copy-start(pred[1024]{0:T(1024)(128)(4,1)S(1)} %get-tuple-element.430) | copy-start | bytes 3076
  95.2 84.0 %copy-start.156 = (pred[8,128]{1,0:T(8,128)(4,1)}, pred[8,128]{1,0:T(8,128)(4,1)S(1)}, u32[]{:S(2)}) copy-start(pred[8,128]{1,0:T(8,128)(4,1)S(1)} %get-tuple-element.423) | copy-start | bytes 3076
  137.5 169.2 %copy-start.45 = (bf16[1024,64]{1,0:T(8,128)(2,1)}, bf16[1024,64]{1,0:T(8,128)(2,1)S(1)}, u32[]{:S(2)}) copy-start(bf16[1024,64]{1,0:T(8,128)(2,1)S(1)} %all_gather.54) | copy-start | bytes 393220
  177.3 129.4 %copy-start.47 = (bf16[1024,64]{1,0:T(8,128)(2,1)}, bf16[1024,64]{1,0:T(8,128)(2,1)S(1)}, u32[]{:S(2)}) copy-start(bf16[1024,64]{1,0:T(8,128)(2,1)S(1)} %all_gather.53) | copy-start | bytes 393220
  261.8 54.3 %copy-start.34 = (bf16[1024,256]{1,0:T(8,128)(2,1)}, bf16[1024,256]{1,0:T(8,128)(2,1)S(1)}, u32[]{:S(2)}) copy-start(bf16[1024,256]{1,0:T(8,128)(2,1)S(1)} %all_gather.55) | copy-start | bytes 1572868
  261.8 44.9 %copy-start.161 = (f32[32]{0:T(128)S(1)}, f32[32]{0:T(128)}, u32[]{:S(2)}) copy-start(f32[32]{0:T(128)} %multiply_power_fusion) | copy-start | bytes 388
  261.8 46.1 %copy-start.102 = (pred[8,128]{0,1:T(8,128)(4,1)S(1)}, pred[8,128]{0,1:T(8,128)(4,1)}, u32[]{:S(2)}) copy-start(pred[8,128]{0,1:T(8,128)(4,1)} %copy.242) | copy-start | bytes 3076
  319.9 41.4 %copy-start.22 = (f32[1024,128]{1,0:T(8,128)}, f32[1024,128]{1,0:T(8,128)S(1)}, u32[]{:S(2)}) copy-start(f32[1024,128]{1,0:T(8,128)S(1)} %get-tuple-element.404) | copy-start | bytes 1572868
  319.9 88.7 %copy-start.20 = (f32[1024,128]{1,0:T(8,128)}, f32[1024,128]{1,0:T(8,128)S(1)}, u32[]{:S(2)}) copy-start(f32[1024,128]{1,0:T(8,128)S(1)} %get-tuple-element.405) | copy-start | bytes 1572868
  451.9 83.8 %all-gather.16.cloned.1.call-start = ((), (), s32[]{:S(2)}) async-start(), calls=%async_computation.17 | async-start | bytes 2228224 | tf_op jit(solution)/shard_map/all_gather | solution.py:216
  452.5 145.6 %all-gather.14.cloned.1.call-start = ((), (), s32[]{:S(2)}) async-start(), calls=%async_computation.16 | async-start | bytes 2228224 | tf_op jit(solution)/shard_map/all_gather | solution.py:215
  453.0 207.6 %all-gather.18.cloned.1.call-start = ((), (), s32[]{:S(2)}) async-start(), calls=%async_computation.18 | async-start | bytes 2228224 | tf_op jit(solution)/shard_map/all_gather | solution.py:217
  453.8 243.9 %all-reduce.35.cloned.1.call-start = ((), (), s32[]{:S(2)}) async-start(), calls=%async_computation.19 | async-start | bytes 4194304 | tf_op jit(solution)/shard_map/psum | solution.py:351
  473.3 229.1 %copy-start.96 = (f32[1024]{0:T(1024)}, f32[1024]{0:T(1024)S(1)}, u32[]{:S(2)}) copy-start(f32[1024]{0:T(1024)S(1)} %get-tuple-element.418) | copy-start | bytes 12292
  473.3 229.1 %copy-start.111 = (f32[1024]{0:T(1024)}, f32[1024]{0:T(1024)S(1)}, u32[]{:S(2)}) copy-start(f32[1024]{0:T(1024)S(1)} %get-tuple-element.417) | copy-start | bytes 12292
  677.7 297.1 %all-reduce.37.cloned.1.call-start = ((), (), s32[]{:S(2)}) async-start(), calls=%async_computation.32 | async-start | bytes 9437184 | tf_op jit(solution)/shard_map/psum | solution.py:309
  923.2 110.6 %reduce-scatter.37.cloned.1.call-start = ((), (), s32[]{:S(2)}) async-start(), calls=%async_computation.31 | async-start | bytes 557056
  926.3 195.2 %reduce-scatter.27.cloned.1.call-start = ((), (), s32[]{:S(2)}) async-start(), calls=%async_computation.26 | async-start | bytes 557056 | tf_op jit(solution)/shard_map/reduce_scatter | solution.py:466
  928.0 257.4 %reduce-scatter.25.cloned.1.call-start = ((), (), s32[]{:S(2)}) async-start(), calls=%async_computation.25 | async-start | bytes 557056 | tf_op jit(solution)/shard_map/reduce_scatter | solution.py:465
  929.6 332.6 %reduce-scatter.29.cloned.1.call-start = ((), (), s32[]{:S(2)}) async-start(), calls=%async_computation.27 | async-start | bytes 1114112 | tf_op jit(solution)/shard_map/reduce_scatter | solution.py:467
  933.8 405.4 %reduce-scatter.23.cloned.1.call-start = ((), (), s32[]{:S(2)}) async-start(), calls=%async_computation.24 | async-start | bytes 1114112 | tf_op jit(solution)/shard_map/reduce_scatter | solution.py:464
  935.6 497.8 %reduce-scatter.35.cloned.1.call-start = ((), (), s32[]{:S(2)}) async-start(), calls=%async_computation.30 | async-start | bytes 4456448 | tf_op jit(solution)/shard_map/reduce_scatter | solution.py:470
  942.5 588.4 %reduce-scatter.31.cloned.1.call-start = ((), (), s32[]{:S(2)}) async-start(), calls=%async_computation.28 | async-start | bytes 4456448 | tf_op jit(solution)/shard_map/reduce_scatter | solution.py:468
  949.9 678.4 %reduce-scatter.33.cloned.1.call-start = ((), (), s32[]{:S(2)}) async-start(), calls=%async_computation.29 | async-start | bytes 4456448 | tf_op jit(solution)/shard_map/reduce_scatter | solution.py:469
  957.1 806.9 %reduce-scatter.21.cloned.1.call-start = ((), (), s32[]{:S(2)}) async-start(), calls=%async_computation.23 | async-start | bytes 3342336 | tf_op jit(solution)/shard_map/reduce_scatter | solution.py:463
  964.0 935.7 %reduce-scatter.15.cloned.1.call-start = ((), (), s32[]{:S(2)}) async-start(), calls=%async_computation.20 | async-start | bytes 3342336 | tf_op jit(solution)/shard_map/reduce_scatter | solution.py:459
  969.0 1065.9 %reduce-scatter.17.cloned.1.call-start = ((), (), s32[]{:S(2)}) async-start(), calls=%async_computation.21 | async-start | bytes 3342336 | tf_op jit(solution)/shard_map/reduce_scatter | solution.py:460
  974.2 1140.5 %reduce-scatter.19.cloned.1.call-start = ((), (), s32[]{:S(2)}) async-start(), calls=%async_computation.22 | async-start | bytes 1114112 | tf_op jit(solution)/shard_map/reduce_scatter | solution.py:462
  979.6 55.6 %copy-start.83 = (bf16[1024,256]{1,0:T(8,128)(2,1)S(1)}, bf16[1024,256]{1,0:T(8,128)(2,1)}, u32[]{:S(2)}) copy-start(bf16[1024,256]{1,0:T(8,128)(2,1)} %all_gather.50) | copy-start | bytes 1572868
  979.6 55.6 %copy-start.122 = (f32[1024]{0:T(1024)S(1)}, f32[1024]{0:T(1024)}, u32[]{:S(2)}) copy-start(f32[1024]{0:T(1024)} %copy-done.121) | copy-start | bytes 12292
  979.7 55.6 %copy-start.138 = (f32[1024]{0:T(1024)S(1)}, f32[1024]{0:T(1024)}, u32[]{:S(2)}) copy-start(f32[1024]{0:T(1024)} %param.31) | copy-start | bytes 12292
  1035.3 78.8 %copy-start.5 = (bf16[1024,1024]{1,0:T(8,128)(2,1)S(1)}, bf16[1024,1024]{1,0:T(8,128)(2,1)}, u32[]{:S(2)}) copy-start(bf16[1024,1024]{1,0:T(8,128)(2,1)} %param.29) | copy-start | bytes 6291460
  1035.3 78.8 %copy-start.97 = (f32[1024]{0:T(1024)S(1)}, f32[1024]{0:T(1024)}, u32[]{:S(2)}) copy-start(f32[1024]{0:T(1024)} %copy-done.96) | copy-start | bytes 12292
  1035.3 78.8 %copy-start.99 = (f32[1024]{0:T(1024)S(1)}, f32[1024]{0:T(1024)}, u32[]{:S(2)}) copy-start(f32[1024]{0:T(1024)} %param.49) | copy-start | bytes 12292
  1035.3 78.8 %copy-start.112 = (f32[1024]{0:T(1024)S(1)}, f32[1024]{0:T(1024)}, u32[]{:S(2)}) copy-start(f32[1024]{0:T(1024)} %copy-done.111) | copy-start | bytes 12292
  1035.3 78.8 %copy-start.120 = (f32[1024]{0:T(1024)S(1)}, f32[1024]{0:T(1024)}, u32[]{:S(2)}) copy-start(f32[1024]{0:T(1024)} %copy-done.119) | copy-start | bytes 12292
  1035.4 78.8 %copy-start.135 = (f32[1024]{0:T(1024)S(1)}, f32[1024]{0:T(1024)}, u32[]{:S(2)}) copy-start(f32[1024]{0:T(1024)} %get-tuple-element.415) | copy-start | bytes 12292
  (160 other events, 694.4 us)
Sparse Core Ops, SparseCore 0:
  10.8 60.6 all-gather.7
  74.2 57.5 all-gather.9
  134.6 58.7 all-gather.11
  452.0 18.7 all-reduce.32
  473.8 61.8 all-gather.15
  538.7 59.3 all-gather.13
  601.3 59.3 all-gather.17
  677.8 19.8 all-reduce.34
  923.3 30.5 all-reduce.36
  956.0 77.6 reduce-scatter.36
  1036.6 72.9 reduce-scatter.26
  1112.4 72.9 reduce-scatter.24
  1188.2 73.9 reduce-scatter.28
  1265.0 74.1 reduce-scatter.22
  1341.9 91.4 reduce-scatter.34
  1436.1 94.6 reduce-scatter.30
  1533.6 94.7 reduce-scatter.32
  1633.8 130.2 reduce-scatter.20
  1769.6 129.9 reduce-scatter.14
  1905.1 129.7 reduce-scatter.16
  2037.7 76.8 reduce-scatter.18
where the time goes:
time: 2130 us; the launch traced here: 2120 us
  waiting for transfers between devices  1250 us (59%)
  blocking collectives  323 us (15%)
  matrix products  240 us (11%)
  other arithmetic  173 us (8%)
  local copies, waits for them, and re-layouts  121 us (6%)
    reduce_scatter x1, waiting for transfers between devices, on_device(): lax.psum_scatter(grad_ssm_output, 'dp', scatter_dimension=1, tiled=True)  136 us
    reduce_scatter x1, waiting for transfers between devices, on_device(): lax.psum_scatter(grad_ssm_gate, 'dp', scatter_dimension=0, tiled=True)  136 us
    reduce_scatter x1, waiting for transfers between devices, on_device(): lax.psum_scatter(grad_ssm_input, 'dp', scatter_dimension=0, tiled=True)  135 us
    reduce_scatter x1, waiting for transfers between devices, on_device(): lax.psum_scatter(feed_shards[1], 'dp', scatter_dimension=0, tiled=True)  97.5 us
    reduce_scatter x1, waiting for transfers between devices, on_device(): lax.psum_scatter(feed_shards[0], 'dp', scatter_dimension=0, tiled=True)  97.5 us
    reduce_scatter x1, waiting for transfers between devices, on_device(): lax.psum_scatter(feed_shards[2], 'dp', scatter_dimension=1, tiled=True)  94.2 us
    reduce_scatter x1, waiting for transfers between devices, on_device(): lax.psum_scatter(grad_state_weight, 'dp', scatter_dimension=0, tiled=True)  79.8 us
    reduce_scatter x1, waiting for transfers between devices, on_device(): lax.psum_scatter(grad_query_weight, 'dp', scatter_dimension=0, tiled=True)  77 us
  transfers between devices with their start and end apart: 21, of which 16 were waited for; matrix products, arithmetic and copies ran while one was open for 13% of the time, Pallas kernels for 0%

commit v1 on v0

--- a/solution.py
+++ b/solution.py
@@ -14,7 +14,70 @@
 epsilon = 1e-05
 rope_base = 100000000000.0
 masked_score = -1e30
-highest_precision = lax.Precision.HIGHEST
+mix_precision = lax.Precision.HIGH
+STEP_PAD = 128
+
+
+def swap_tensor(values):
+    return lax.ppermute(values, "tensor", [(0, 1), (1, 0)])
+
+
+def pair_sum(values):
+    low = lax.reduce_precision(values, 8, 7)
+    return low + swap_tensor(low.astype(jnp.bfloat16)).astype(jnp.float32)
+
+
+def pair_sum_wide(values):
+    return values + swap_tensor(values)
+
+
+def bit_orders(count):
+    bits = list(range(count.bit_length() - 1))
+    return bits, bits[1::-1] + bits[2:]
+
+
+def partners(count, bit):
+    return [(i, i ^ (1 << bit)) for i in range(count)]
+
+
+def gather_rows(shard, order):
+    count = lax.axis_size("dp")
+    place = lax.axis_index("dp")
+    held = shard
+    done = []
+    for bit in reversed(order):
+        other = lax.ppermute(held, "dp", partners(count, bit))
+        low_side = (place >> bit) & 1 == 0
+        axis = sum(earlier > bit for earlier in done)
+        held = jnp.stack(
+            [jnp.where(low_side, held, other), jnp.where(low_side, other, held)], axis=axis
+        )
+        done.append(bit)
+    return held.reshape(count * shard.shape[0], shard.shape[1])
+
+
+def scatter_rows(partial_sum, order):
+    count = lax.axis_size("dp")
+    place = lax.axis_index("dp")
+    rows = partial_sum.shape[0] // count
+    left = sorted(order, reverse=True)
+    held = partial_sum.reshape((2,) * len(left) + (rows, partial_sum.shape[1]))
+    for bit in order:
+        axis = left.index(bit)
+        side = (place >> bit) & 1
+        mine = lax.dynamic_index_in_dim(held, side, axis, keepdims=False)
+        theirs = lax.dynamic_index_in_dim(held, 1 - side, axis, keepdims=False)
+        came = lax.ppermute(theirs.astype(jnp.bfloat16), "dp", partners(count, bit))
+        held = mine + came.astype(jnp.float32)
+        left.remove(bit)
+    return held
+
+
+def sum_all(vector):
+    count = lax.axis_size("dp")
+    for bit in range(count.bit_length() - 1):
+        vector = vector + lax.ppermute(vector, "dp", partners(count, bit))
+    return vector
 
 
 def forward_dot(left, right):
@@ -81,22 +144,26 @@
     sequence_length, head_count, head_width = heads_in.shape
     block_count = sequence_length // BLK
     states = state_in.shape[1]
-    cumulative = jnp.cumsum(
-        (-step_size * rate[None, :]).reshape(block_count, BLK, head_count), axis=1
-    ).transpose(0, 2, 1)
+    offsets = jnp.arange(BLK)
+    lower = (offsets[:, None] >= offsets[None, :]).astype(jnp.float32)
+    cumulative = jnp.einsum(
+        "ts,nsh->nht",
+        lower,
+        (-step_size * rate[None, :]).reshape(block_count, BLK, head_count),
+        precision=lax.Precision.HIGHEST,
+    )
     block_ids = segment_ids.reshape(block_count, BLK)
     scaled_in = (heads_in * step_size[:, :, None]).reshape(block_count, BLK, head_count, head_width)
     in_blocks = state_in.reshape(block_count, BLK, states)
     out_blocks = state_out.reshape(block_count, BLK, states)
-    offsets = jnp.arange(BLK)
     allowed = (offsets[:, None] >= offsets[None, :])[None] & (
         block_ids[:, :, None] == block_ids[:, None, :]
     )
     spread = cumulative[:, :, :, None] - cumulative[:, :, None, :]
     decays = jnp.where(allowed[:, None], jnp.exp(jnp.where(allowed[:, None], spread, 0.0)), 0.0)
-    intersection = jnp.einsum("ntk,nsk->nts", out_blocks, in_blocks, precision=highest_precision)
+    intersection = jnp.einsum("ntk,nsk->nts", out_blocks, in_blocks, precision=mix_precision)
     inside = jnp.einsum(
-        "nhts,nshp->nthp", decays * intersection[:, None], scaled_in, precision=highest_precision
+        "nhts,nshp->nthp", decays * intersection[:, None], scaled_in, precision=mix_precision
     )
     last_ids = block_ids[:, -1]
     to_end = jnp.where(
@@ -105,24 +172,23 @@
         0.0,
     )
     local_state = jnp.einsum(
-        "nhs,nshp,nsk->nhpk", to_end, scaled_in, in_blocks, precision=highest_precision
+        "nhs,nshp,nsk->nhpk", to_end, scaled_in, in_blocks, precision=mix_precision
     )
     carried = jnp.concatenate([jnp.zeros((1,), dtype=bool), last_ids[1:] == last_ids[:-1]])
 
-    def advance(running, pieces):
-        fresh_state, factor, keep_going = pieces
-        return (jnp.where(keep_going, factor[:, None, None] * running, 0.0) + fresh_state, running)
-
-    start_state = jnp.zeros(local_state.shape[1:], local_state.dtype)
-    _, entering = lax.scan(
-        advance, start_state, (local_state, jnp.exp(cumulative[:, :, -1]), carried)
-    )
+    factors = jnp.where(carried[:, None], jnp.exp(cumulative[:, :, -1]), 0.0)
+    running = jnp.zeros(local_state.shape[1:], local_state.dtype)
+    entering = [running]
+    for block in range(block_count - 1):
+        running = factors[block][:, None, None] * running + local_state[block]
+        entering.append(running)
+    entering = jnp.stack(entering)
     earlier_ids = jnp.concatenate([jnp.full((1,), -1, jnp.int32), last_ids[:-1]])
     from_start = jnp.where(
         (block_ids == earlier_ids[:, None])[:, None, :], jnp.exp(cumulative), 0.0
     )
     across = (
-        jnp.einsum("ntk,nhpk->nthp", out_blocks, entering, precision=highest_precision)
+        jnp.einsum("ntk,nhpk->nthp", out_blocks, entering, precision=mix_precision)
         * from_start.transpose(0, 2, 1)[:, :, :, None]
     )
     return (inside + across).reshape(sequence_length, head_count, head_width)
@@ -202,44 +268,40 @@
 ):
     segment_ids = segments.reshape(-1)
     sequence_length = inputs.shape[0]
-    gathered = (
-        lax.all_gather(ssm_gate, "dp", axis=0, tiled=True),
-        lax.all_gather(ssm_input, "dp", axis=0, tiled=True),
-        lax.all_gather(step_weight, "dp", axis=0, tiled=True),
-        lax.all_gather(state_weight, "dp", axis=0, tiled=True),
-        lax.all_gather(query_weight, "dp", axis=0, tiled=True),
-        lax.all_gather(key_matrix, "dp", axis=0, tiled=True),
-        lax.all_gather(value_matrix, "dp", axis=0, tiled=True),
-        lax.all_gather(ssm_output, "dp", axis=1, tiled=True),
-        lax.all_gather(output_weight, "dp", axis=1, tiled=True),
-        lax.all_gather(gate_weight, "dp", axis=0, tiled=True),
-        lax.all_gather(up_weight, "dp", axis=0, tiled=True),
-        lax.all_gather(down_weight, "dp", axis=1, tiled=True),
-    )
-    (
-        full_gate,
-        full_input,
-        full_step,
-        full_state,
-        full_query,
-        full_key,
-        full_value,
-        full_ssm_out,
-        full_output,
-        full_feed_gate,
-        full_feed_up,
-        full_down,
-    ) = gathered
+    order_a, order_b = bit_orders(lax.axis_size("dp"))
+    inner_width = ssm_input.shape[1]
+    step_width = step_weight.shape[1]
+    query_width = query_weight.shape[1]
+    key_width = key_matrix.shape[1]
+    main_width = inner_width + STEP_PAD
+    step_padding = ((0, 0), (0, STEP_PAD - step_width))
+    side_a = gather_rows(
+        jnp.concatenate([ssm_input, jnp.pad(step_weight, step_padding), state_weight], axis=1),
+        order_a,
+    )
+    side_b = gather_rows(
+        jnp.concatenate([ssm_gate, query_weight, key_matrix, value_matrix], axis=1), order_b
+    )
+    mixer_out_local = jnp.concatenate([ssm_output, output_weight], axis=0).T
+    mixer_out_local, gate_local, up_local, down_local, side_a, side_b = lax.optimization_barrier(
+        (mixer_out_local, gate_weight, up_weight, down_weight.T, side_a, side_b)
+    )
+    mixer_out = gather_rows(mixer_out_local, order_a)
+    full_down = gather_rows(down_local, order_b)
+    full_feed_gate = gather_rows(gate_local, order_a)
+    full_feed_up = gather_rows(up_local, order_b)
     tokens = inputs.astype(jnp.float32)
     first_scale = rms_scale(tokens)
     hidden_activations = (tokens * first_scale * mixer_gain).astype(jnp.bfloat16)
-    gate_z = forward_dot(hidden_activations, full_gate)
-    inner_raw = forward_dot(hidden_activations, full_input)
-    step_raw = forward_dot(hidden_activations, full_step)
-    state_raw = forward_dot(hidden_activations, full_state)
-    query_raw = forward_dot(hidden_activations, full_query)
-    key_raw = forward_dot(hidden_activations, full_key)
-    value_raw = forward_dot(hidden_activations, full_value)
+    raw_a = forward_dot(hidden_activations, side_a)
+    raw_b = forward_dot(hidden_activations, side_b)
+    inner_raw = raw_a[:, :inner_width]
+    step_raw = raw_a[:, inner_width : inner_width + step_width]
+    state_raw = raw_a[:, main_width:]
+    gate_z = raw_b[:, :inner_width]
+    query_raw, key_raw, value_raw = jnp.split(
+        raw_b[:, inner_width:], [query_width, query_width + key_width], axis=1
+    )
     state_conv, state_pull = jax.vjp(
         partial(causal_conv, segment_ids), state_raw, conv_state, state_bias
     )
@@ -255,7 +317,7 @@
         decay_log,
         skip_gain,
     )
-    all_squares = lax.psum(jnp.sum(gated_ssm * gated_ssm, axis=-1, keepdims=True), "tensor")
+    all_squares = pair_sum_wide(jnp.sum(gated_ssm * gated_ssm, axis=-1, keepdims=True))
     ssm_scale = lax.rsqrt(all_squares / (HM * HEAD_SIZE) + epsilon)
     normed = (gated_ssm * ssm_scale * ssm_norm).astype(jnp.bfloat16)
     local_kv = key_raw.shape[1] // HEAD_SIZE
@@ -299,75 +361,41 @@
     attention_result = (
         jnp.concatenate(attended_parts, axis=0).reshape(sequence_length, -1).astype(jnp.bfloat16)
     )
-    mixer_part = forward_dot(normed, full_ssm_out) + forward_dot(attention_result, full_output)
-    middle = tokens + lax.psum(mixer_part.astype(jnp.bfloat16), "tensor").astype(jnp.float32)
+    mixer_in = jnp.concatenate([normed, attention_result], axis=1)
+    middle = tokens + pair_sum(back_dot(mixer_in, mixer_out))
     second_scale = rms_scale(middle)
     hidden_two = (middle * second_scale * feed_gain).astype(jnp.bfloat16)
     gate_value = forward_dot(hidden_two, full_feed_gate)
     up_value = forward_dot(hidden_two, full_feed_up)
     product = (jax.nn.silu(gate_value) * up_value).astype(jnp.bfloat16)
-    feed_out = lax.psum(forward_dot(product, full_down).astype(jnp.bfloat16), "tensor").astype(
-        jnp.float32
-    )
+    feed_out = pair_sum(back_dot(product, full_down))
     output = (middle + feed_out).astype(jnp.bfloat16)
-    regathered = (
-        lax.all_gather(ssm_gate, "dp", axis=0, tiled=True),
-        lax.all_gather(ssm_input, "dp", axis=0, tiled=True),
-        lax.all_gather(step_weight, "dp", axis=0, tiled=True),
-        lax.all_gather(state_weight, "dp", axis=0, tiled=True),
-        lax.all_gather(query_weight, "dp", axis=0, tiled=True),
-        lax.all_gather(key_matrix, "dp", axis=0, tiled=True),
-        lax.all_gather(value_matrix, "dp", axis=0, tiled=True),
-        lax.all_gather(ssm_output, "dp", axis=1, tiled=True),
-        lax.all_gather(output_weight, "dp", axis=1, tiled=True),
-        lax.all_gather(gate_weight, "dp", axis=0, tiled=True),
-        lax.all_gather(up_weight, "dp", axis=0, tiled=True),
-        lax.all_gather(down_weight, "dp", axis=1, tiled=True),
-    )
-    (
-        back_gate,
-        back_input,
-        back_step,
-        back_state,
-        back_query,
-        back_key,
-        back_value,
-        back_ssm_out,
-        back_output,
-        back_feed_gate,
-        back_feed_up,
-        back_down,
-    ) = regathered
-    grad_down_weight = outer_sum(product, upstream)
-    grad_product = back_dot(upstream, back_down)
+    down_shard = scatter_rows(outer_sum(upstream, product), order_b).T
+    grad_product = forward_dot(upstream, full_down)
     gate_sigmoid = jax.nn.sigmoid(gate_value)
     grad_gate = (
         grad_product * up_value * gate_sigmoid * (1.0 + gate_value * (1.0 - gate_sigmoid))
     ).astype(jnp.bfloat16)
     grad_up = (grad_product * jax.nn.silu(gate_value)).astype(jnp.bfloat16)
-    grad_gate_weight = outer_sum(hidden_two, grad_gate)
-    grad_up_weight = outer_sum(hidden_two, grad_up)
-    feed_shards = (grad_gate_weight, grad_up_weight, grad_down_weight)
-    grad_hidden_two = lax.psum(
-        (back_dot(grad_gate, back_feed_gate) + back_dot(grad_up, back_feed_up)).astype(
-            jnp.bfloat16
-        ),
-        "tensor",
-    ).astype(jnp.float32)
+    feed_gate_shard = scatter_rows(outer_sum(hidden_two, grad_gate), order_a)
+    feed_up_shard = scatter_rows(outer_sum(hidden_two, grad_up), order_b)
+    grad_hidden_two = pair_sum(
+        back_dot(grad_gate, full_feed_gate) + back_dot(grad_up, full_feed_up)
+    )
     grad_mid_norm, grad_feed_gain = norm_back(middle, second_scale, feed_gain, grad_hidden_two)
     grad_middle = upstream.astype(jnp.float32) + grad_mid_norm
     grad_branch = grad_middle.astype(jnp.bfloat16)
-    grad_ssm_output = outer_sum(normed, grad_branch)
-    grad_output_weight = outer_sum(attention_result, grad_branch)
-    grad_normed = back_dot(grad_branch, back_ssm_out)
+    mixer_out_shard = scatter_rows(outer_sum(grad_branch, mixer_in), order_a).T
+    grad_mixer_in = forward_dot(grad_branch, mixer_out)
+    grad_normed = grad_mixer_in[:, :inner_width]
     grad_attended = (
-        back_dot(grad_branch, back_output)
+        grad_mixer_in[:, inner_width:]
         .astype(jnp.bfloat16)
         .reshape(sequence_length, local_kv, group_size, HEAD_SIZE)
     )
     scaled_grad = grad_normed * ssm_norm
     grad_ssm_norm = jnp.sum(grad_normed * gated_ssm * ssm_scale, axis=0)
-    cross_sum = lax.psum(jnp.sum(scaled_grad * gated_ssm, axis=-1, keepdims=True), "tensor")
+    cross_sum = pair_sum_wide(jnp.sum(scaled_grad * gated_ssm, axis=-1, keepdims=True))
     grad_gated = ssm_scale * scaled_grad - gated_ssm * ssm_scale**3 * cross_sum / (HM * HEAD_SIZE)
     (
         grad_inner,
@@ -428,87 +456,74 @@
         .astype(jnp.bfloat16)
     )
     grad_value = grad_value_sum.reshape(sequence_length, -1).astype(jnp.bfloat16)
-    grad_z_low = grad_gate_z.astype(jnp.bfloat16)
-    grad_inner_low = grad_inner.astype(jnp.bfloat16)
-    grad_step_low = grad_step_raw.astype(jnp.bfloat16)
-    grad_ssm_gate = outer_sum(hidden_activations, grad_z_low)
-    grad_ssm_input = outer_sum(hidden_activations, grad_inner_low)
-    grad_step_weight = outer_sum(hidden_activations, grad_step_low)
-    grad_query_weight = outer_sum(hidden_activations, grad_query)
-    grad_key_weight = outer_sum(hidden_activations, grad_key)
-    grad_value_weight = outer_sum(hidden_activations, grad_value)
-    partial_hidden = (
-        back_dot(grad_z_low, back_gate)
-        + back_dot(grad_inner_low, back_input)
-        + back_dot(grad_step_low, back_step)
-        + back_dot(grad_query, back_query)
-        + back_dot(grad_key, back_key)
-        + back_dot(grad_value, back_value)
-    )
-    hidden_sum, state_sum = (
-        lax.psum(partial_hidden.astype(jnp.bfloat16), "tensor").astype(jnp.float32),
-        lax.psum(grad_state_conv.astype(jnp.bfloat16), "tensor").astype(jnp.float32),
-    )
+    state_sum = pair_sum(grad_state_conv)
+    grads_b = jnp.concatenate(
+        [grad_gate_z.astype(jnp.bfloat16), grad_query, grad_key, grad_value], axis=1
+    )
+    shard_b = scatter_rows(outer_sum(hidden_activations, grads_b), order_b)
+    grads_main = jnp.concatenate(
+        [
+            grad_inner.astype(jnp.bfloat16),
+            jnp.pad(grad_step_raw.astype(jnp.bfloat16), step_padding),
+        ],
+        axis=1,
+    )
+    hidden_sum = pair_sum(back_dot(grads_b, side_b) + back_dot(grads_main, side_a[:, :main_width]))
     grad_state_raw, grad_conv_state, grad_state_bias = state_pull(state_sum)
     grad_state_low = grad_state_raw.astype(jnp.bfloat16)
-    grad_state_weight = outer_sum(hidden_activations, grad_state_low)
-    grad_hidden = hidden_sum + back_dot(grad_state_low, back_state)
+    shard_a = scatter_rows(
+        outer_sum(hidden_activations, jnp.concatenate([grads_main, grad_state_low], axis=1)),
+        order_a,
+    )
+    grad_hidden = hidden_sum + back_dot(grad_state_low, side_a[:, main_width:])
     grad_in_norm, grad_mixer_gain = norm_back(tokens, first_scale, mixer_gain, grad_hidden)
     grad_inputs = (grad_middle + grad_in_norm).astype(jnp.bfloat16)
-    weight_shards = (
-        lax.psum_scatter(grad_ssm_gate, "dp", scatter_dimension=0, tiled=True),
-        lax.psum_scatter(grad_ssm_input, "dp", scatter_dimension=0, tiled=True),
-        lax.psum_scatter(grad_step_weight, "dp", scatter_dimension=0, tiled=True),
-        lax.psum_scatter(grad_state_weight, "dp", scatter_dimension=0, tiled=True),
-        lax.psum_scatter(grad_ssm_output, "dp", scatter_dimension=1, tiled=True),
-        lax.psum_scatter(grad_query_weight, "dp", scatter_dimension=0, tiled=True),
-        lax.psum_scatter(grad_key_weight, "dp", scatter_dimension=0, tiled=True),
-        lax.psum_scatter(grad_value_weight, "dp", scatter_dimension=0, tiled=True),
-        lax.psum_scatter(grad_output_weight, "dp", scatter_dimension=1, tiled=True),
-        lax.psum_scatter(feed_shards[0], "dp", scatter_dimension=0, tiled=True),
-        lax.psum_scatter(feed_shards[1], "dp", scatter_dimension=0, tiled=True),
-        lax.psum_scatter(feed_shards[2], "dp", scatter_dimension=1, tiled=True),
-    )
-    small_sums = lax.psum(
-        (
-            grad_mixer_gain,
-            grad_conv_input,
-            grad_input_bias,
-            grad_conv_state,
-            grad_state_bias,
-            grad_step_bias,
-            grad_decay_log,
-            grad_skip_gain,
-            grad_ssm_norm,
-            grad_feed_gain,
-        ),
-        "dp",
-    )
+    small_parts = (
+        grad_mixer_gain,
+        grad_conv_input,
+        grad_input_bias,
+        grad_conv_state,
+        grad_state_bias,
+        grad_ssm_norm,
+        grad_feed_gain,
+        grad_step_bias,
+        grad_decay_log,
+        grad_skip_gain,
+    )
+    packed = jnp.concatenate([part.reshape(-1) for part in small_parts])
+    packed = jnp.pad(packed, (0, -packed.shape[0] % 1024)).reshape(-1, 128)
+    packed = sum_all(packed).reshape(-1)
+    small_sums = []
+    first = 0
+    for part in small_parts:
+        small_sums.append(packed[first : first + part.size].reshape(part.shape))
+        first += part.size
+    value_first = inner_width + query_width + key_width
     return (
         output,
         grad_inputs,
         small_sums[0],
-        weight_shards[0],
-        weight_shards[1],
-        weight_shards[2],
-        weight_shards[3],
+        shard_b[:, :inner_width],
+        shard_a[:, :inner_width],
+        shard_a[:, inner_width : inner_width + step_width],
+        shard_a[:, main_width:],
         small_sums[1],
         small_sums[2],
         small_sums[3],
         small_sums[4],
-        small_sums[5],
-        small_sums[6],
         small_sums[7],
         small_sums[8],
-        weight_shards[4],
-        weight_shards[5],
-        weight_shards[6],
-        weight_shards[7],
-        weight_shards[8],
         small_sums[9],
-        weight_shards[9],
-        weight_shards[10],
-        weight_shards[11],
+        small_sums[5],
+        mixer_out_shard[:inner_width],
+        shard_b[:, inner_width : inner_width + query_width],
+        shard_b[:, inner_width + query_width : value_first],
+        shard_b[:, value_first:],
+        mixer_out_shard[inner_width:],
+        small_sums[6],
+        feed_gate_shard,
+        feed_up_shard,
+        down_shard,
     )
 
 

time: 2130 us -> 694 us (0.33)
  waiting for transfers between devices: 1250 us -> 193 us
  blocking collectives: 323 us -> 0 us
  matrix products: 240 us -> 161 us
  starting transfers between devices: 1.6 us -> 74.5 us
  other arithmetic: 173 us -> 138 us
    reduce_scatter x11 -> x0, waiting for transfers between devices: 993 us -> none  [the longest x1 136 us: on_device(): lax.psum_scatter(grad_ssm_output, 'dp', scatter_dimension=1, tiled=True)]
    all_gather x6 -> x0, blocking collectives: 245 us -> none  [the longest x1 43.3 us: on_device(): lax.all_gather(step_weight, 'dp', axis=0, tiled=True)]
    ppermute x0 -> x59, waiting for transfers between devices: none -> 193 us  [the longest x24 100 us: gather_rows(): other = lax.ppermute(held, 'dp', partners(count, bit))]
    all_gather x6 -> x0, waiting for transfers between devices: 172 us -> none  [the longest x1 60.3 us: on_device(): lax.all_gather(up_weight, 'dp', axis=0, tiled=True)]
    psum x3 -> x0, blocking collectives: 78.5 us -> none  [the longest x1 72.9 us: on_device(): lax.psum((grad_mixer_gain, grad_conv_input, grad_input_bias, grad_conv_st...]
    ppermute x0 -> x59, starting transfers between devices: none -> 74.5 us  [the longest x24 38.7 us: scatter_rows(): came = lax.ppermute(theirs.astype(jnp.bfloat16), 'dp', partners(count, bit))]
    unnamed x22 -> x0, waiting for transfers between devices: 56.2 us -> none
    unnamed x384 -> x442, local copies, waits for them, and re-layouts: 22.4 us -> 49.5 us
  transfers between devices with their start and end apart: 21 -> 59, of which waited for: 16 -> 32; matrix products, arithmetic and copies ran while one was open for 13% -> 46% of each run, Pallas kernels for 0% -> 0%
where the time goes in v1:
time: 694 us; the launch traced here: 689 us
  waiting for transfers between devices  193 us (28%)
  matrix products  161 us (23%)
  other arithmetic  138 us (20%)
  local copies, waits for them, and re-layouts  117 us (17%)
  starting transfers between devices  74.5 us (11%)
    ppermute x24, waiting for transfers between devices, gather_rows(): other = lax.ppermute(held, 'dp', partners(count, bit))  100 us
    ppermute x24, waiting for transfers between devices, scatter_rows(): came = lax.ppermute(theirs.astype(jnp.bfloat16), 'dp', partners(count, bit))  89.5 us
    unnamed x442, local copies, waits for them, and re-layouts  49.5 us
    ppermute x24, starting transfers between devices, scatter_rows(): came = lax.ppermute(theirs.astype(jnp.bfloat16), 'dp', partners(count, bit))  38.7 us
    dot_general x7, matrix products, back_dot(): jnp.einsum('tj,ij->ti', grad_rows, weights, preferred_element_type=jnp.fl...  33.7 us
    ppermute x24, starting transfers between devices, gather_rows(): other = lax.ppermute(held, 'dp', partners(count, bit))  29.7 us
    dot_general x6, matrix products, forward_dot(): return jnp.dot(left, right, preferred_element_type=jnp.float32)  23.1 us
    dot_general x3, matrix products, span_mix(): jnp.einsum('nhts,nshp->nthp', decays * intersection[:, None], scaled_in,...  23.1 us
  transfers between devices with their start and end apart: 59, of which 32 were waited for; matrix products, arithmetic and copies ran while one was open for 46% of the time, Pallas kernels for 0%

profile of v1, /device:TPU:0, one launch (start us, length us, event | category | flops | bytes accessed | tf_op | source)
XLA Modules:
  0.0 688.6 jit_solution(10027812185492123208)
XLA Ops:
  23.0 7.2 %collective-permute-done.5 = bf16[2,64,1152]{2,1,0:T(8,128)(2,1)S(1)} collective-permute-done((bf16[2,64,1152]{2,1,0:T(8,128)(2,1)S(1)}, bf16[2,64,1152]{2,1,0:T(8,128)(2,1)S(1)}, u32[]{:S(2)}, u32[]{:S(2)}) %collective-permute-start.5) | collective-permute-done | bytes 294944 | tf_op jit(solution)/shard_map/ppermute | solution.py:49
  37.6 5.2 collective-permute-done.6
  45.3 7.3 %collective-permute-done.2 = bf16[2,2,64,1152]{3,2,1,0:T(8,128)(2,1)} collective-permute-done((bf16[2,2,64,1152]{3,2,1,0:T(8,128)(2,1)}, bf16[2,2,64,1152]{3,2,1,0:T(8,128)(2,1)}, u32[]{:S(2)}, u32[]{:S(2)}) %collective-permute-start.2) | collective-permute-done | bytes 589856 | tf_op jit(solution)/shard_map/ppermute | solution.py:49
  58.8 4.4 copy.417
  64.5 11.0 %collective-permute-done.7 = bf16[2,2,2,64,1152]{4,3,0,1,2:T(8,128)(2,1)} collective-permute-done((bf16[2,2,2,64,1152]{4,3,0,1,2:T(8,128)(2,1)}, bf16[2,2,2,64,1152]{4,3,0,1,2:T(8,128)(2,1)}, u32[]{:S(2)}, u32[]{:S(2)}) %collective-permute-start.7) | collective-permute-done | bytes 1179680 | tf_op jit(solution)/shard_map/ppermute | solution.py:49
  114.7 9.6 %fusion.69 = (f32[1024,768]{1,0:T(8,128)}, f32[1024,768]{1,0:T(8,128)}) fusion(f32[1024,768]{1,0:T(8,128)} %slice.357, pred[1024]{0:T(1024)(128)(4,1)S(1)} %get-tuple-element.330, f32[768]{0:T(1024)S(1)} %copy-done.122, pred[1024]{0:T(1024)(128)(4,1)S(1)} %get-tuple-element.331, f32[768]{0:T(1024)S(1)} %copy-done.124, ...), kind=kLoop, calls=%fused_computation.135 | loop fusion | flops 11796480 | bytes 9455616 | tf_op jit(solution)/shard_map/jvp(jit(silu))/mul | solution.py:117
  141.0 7.9 %bitcast_add_fusion.1 = f32[8,128,12,64]{1,3,2,0:T(8,128)S(1)} fusion(f32[8,128,12,64]{1,3,2,0:T(8,128)S(1)} %fusion.291, f32[8,128,128]{2,1,0:T(8,128)S(1)} %fusion.290, f32[8,12,128]{2,1,0:T(8,128)S(1)} %fusion.220, pred[8,128,128]{2,1,0:T(8,128)(4,1)S(1)} %copy-done.107, f32[8,128,12,64]{1,0,3,2:T(8,128)S(1)} %bitcast.706, ...), kind=kOutput, calls=%fused_computation.105 | convolution fusion | flops 612630528 | bytes 10240000 | tf_op jit(solution)/shard_map/jvp(nhts,nshp->nthp)/dot_general | solution.py:165
  157.2 5.9 multiply_reduce_fusion.13
  193.4 10.6 %collective-permute-done.10 = bf16[2,64,1024]{2,1,0:T(8,128)(2,1)S(1)} collective-permute-done((bf16[2,64,1024]{2,1,0:T(8,128)(2,1)S(1)}, bf16[2,64,1024]{2,1,0:T(8,128)(2,1)S(1)}, u32[]{:S(2)}, u32[]{:S(2)}) %collective-permute-start.10) | collective-permute-done | bytes 262176 | tf_op jit(solution)/shard_map/ppermute | solution.py:49
  209.6 6.5 collective-permute-done.11
  222.5 8.4 %collective-permute-done.24 = bf16[2,2,64,1024]{3,2,0,1:T(8,128)(2,1)S(1)} collective-permute-done((bf16[2,2,64,1024]{3,2,0,1:T(8,128)(2,1)S(1)}, bf16[2,2,64,1024]{3,2,0,1:T(8,128)(2,1)S(1)}, u32[]{:S(2)}, u32[]{:S(2)}) %collective-permute-start.24) | collective-permute-done | bytes 524320 | tf_op jit(solution)/shard_map/ppermute | solution.py:49
  233.6 19.7 %collective-permute-done.12 = bf16[2,2,2,64,1024]{4,3,2,1,0:T(8,128)(2,1)S(1)} collective-permute-done((bf16[2,2,2,64,1024]{4,3,2,1,0:T(8,128)(2,1)S(1)}, bf16[2,2,2,64,1024]{4,3,2,1,0:T(8,128)(2,1)S(1)}, u32[]{:S(2)}, u32[]{:S(2)}) %collective-permute-start.12) | collective-permute-done | bytes 1048608 | tf_op jit(solution)/shard_map/ppermute | solution.py:49
  254.5 5.1 reduce-precision_convert_fusion.1
  265.6 8.0 %collective-permute-done.17 = bf16[2,2,2,64,1024]{4,3,2,1,0:T(8,128)(2,1)} collective-permute-done((bf16[2,2,2,64,1024]{4,3,2,1,0:T(8,128)(2,1)}, bf16[2,2,2,64,1024]{4,3,2,1,0:T(8,128)(2,1)}, u32[]{:S(2)}, u32[]{:S(2)}) %collective-permute-start.17) | collective-permute-done | bytes 1048608 | tf_op jit(solution)/shard_map/ppermute | solution.py:49
  281.6 4.4 fusion.298
  291.8 5.7 fusion.37
  317.0 5.7 fusion.283
  323.2 6.8 collective-permute-done.55
  332.0 17.3 %collective-permute-done.51 = bf16[2,2,2,64,1024]{4,3,0,1,2:T(8,128)(2,1)S(1)} collective-permute-done((bf16[2,2,2,64,1024]{4,3,0,1,2:T(8,128)(2,1)S(1)}, bf16[2,2,2,64,1024]{4,3,0,1,2:T(8,128)(2,1)S(1)}, u32[]{:S(2)}, u32[]{:S(2)}) %collective-permute-start.51) | collective-permute-done | bytes 1048608 | tf_op jit(solution)/shard_map/ppermute | solution.py:70
  352.7 7.9 %collective-permute-done.52 = bf16[2,2,64,1024]{3,2,0,1:T(8,128)(2,1)S(1)} collective-permute-done((bf16[2,2,64,1024]{3,2,0,1:T(8,128)(2,1)S(1)}, bf16[2,2,64,1024]{3,2,0,1:T(8,128)(2,1)S(1)}, u32[]{:S(2)}, u32[]{:S(2)}) %collective-permute-start.52) | collective-permute-done | bytes 524320 | tf_op jit(solution)/shard_map/ppermute | solution.py:70
  363.3 7.0 %collective-permute-start.58 = (bf16[64,1024]{1,0:T(8,128)(2,1)S(1)}, bf16[64,1024]{1,0:T(8,128)(2,1)S(1)}, u32[]{:S(2)}, u32[]{:S(2)}) collective-permute-start(bf16[64,1024]{1,0:T(8,128)(2,1)S(1)} %fusion.205), channel_id=1, source_target_pairs={{0,16},{2,18},{4,20},{6,22},{8,24},{10,26},{12,28},{14,30},{16,0},... | collective-permute-start | bytes 393224 | tf_op jit(solution)/shard_map/ppermute | solution.py:70
  370.3 7.9 %collective-permute-start.54 = (bf16[64,1024]{1,0:T(8,128)(2,1)S(1)}, bf16[64,1024]{1,0:T(8,128)(2,1)S(1)}, u32[]{:S(2)}, u32[]{:S(2)}) collective-permute-start(bf16[64,1024]{1,0:T(8,128)(2,1)S(1)} %fusion.204), channel_id=1, source_target_pairs={{0,16},{2,18},{4,20},{6,22},{8,24},{10,26},{12,28},{14,30},{16,0},... | collective-permute-start | bytes 393224 | tf_op jit(solution)/shard_map/ppermute | solution.py:70
  381.8 4.9 collective-permute-done.54
  390.9 5.4 subtract_add_fusion
  396.3 4.4 fusion.108
  400.7 4.4 fusion.284
  405.4 4.9 fusion.125
  410.3 5.4 fusion.3
  426.5 5.4 fusion
  431.9 5.4 fusion.146
  453.1 8.3 %multiply_reduce_fusion.5 = (f32[768]{0:T(1024)}, f32[1024,768]{1,0:T(8,128)}, bf16[1024,768]{1,0:T(8,128)(2,1)}) fusion(f32[1024,768]{1,0:T(8,128)S(1)} %copy-done.4, f32[1024,1152]{1,0:T(8,128)} %copy-done.18, f32[1024]{0:T(1024)S(1)} %bitcast.780, f32[1024,768]{1,0:T(8,128)} %get-tuple-element.211, f32[1024]{0:T(1024)} %bitcast.781, ...), kind=kLoop, calls=%fused_computation.108 | loop fusion | flops 21232896 | bytes 20468736 | tf_op jit(solution)/shard_map/transpose(jvp())/reduce_sum | solution.py:223
  478.5 5.0 multiply_reduce_fusion.4
  487.2 5.0 concatenate.86
  492.2 7.5 %fusion.260 = f32[1024,1152]{1,0:T(8,128)} fusion(bf16[1024,1152]{1,0:T(8,128)(2,1)} %concatenate.86, bf16[1024,1024]{0,1:T(8,128)(2,1)} %copy-done.2, f32[1024]{0:T(1024)S(1)} %copy-done.143, f32[1024]{0:T(1024)S(1)} %copy-done.127), kind=kOutput, calls=%fused_computation.572 | convolution fusion | flops 2420113408 | bytes 9183232 | tf_op jit(solution)/shard_map/ti,tj->ij/dot_general | solution.py:92
  499.7 4.4 fusion.294
  504.1 10.7 %fusion.46 = (f32[8,12,128]{2,1,0:T(8,128)}, f32[8,12,128]{2,1,0:T(8,128)}, f32[8,128,128]{2,1,0:T(8,128)}) fusion(f32[8,128,128]{2,1,0:T(8,128)S(1)} %copy-done.87, f32[8,12,128]{2,1,0:T(8,128)S(1)} %copy-done.65, pred[8,128,128]{2,1,0:T(8,128)(4,1)S(1)} %copy-done.108, f32[8,128,12,64]{1,0,3,2:T(8,128)S(1)} %bitcast.709, ...), kind=kOutput, calls=%fused_computation.81 | convolution fusion | flops 621912064 | bytes 7667712 | tf_op jit(solution)/shard_map/transpose(jvp(nhts,nshp->nthp))/dot_general | solution.py:165
  514.9 4.5 bitcast_add_fusion
  527.8 11.0 %fusion.266 = (f32[768]{0:T(1024)}, f32[768]{0:T(1024)}, f32[768]{0:T(1024)}, f32[768]{0:T(1024)}, f32[768]{0:T(1024)}, /*index=5*/f32[1024,768]{1,0:T(8,128)S(1)}) fusion(f32[1024,1152]{1,0:T(8,128)} %copy-done.17, f32[1024,768]{1,0:T(8,128)} %slice.357, pred[1024]{0:T(1024)(128)(4,1)S(1)} %copy-done.118, pred[1024]{0:T(1024)(128)(4,1)S(1)} %copy-done.114, ...), kind=kLoop, calls=%fused_computation.575 | loop fusion | flops 18870528 | bytes 22041600 | tf_op jit(solution)/shard_map/transpose(jvp())/reduce_sum | solution.py:110
  538.9 5.2 multiply_select_fusion.1
  567.2 5.1 fusion.285
  592.6 8.5 %collective-permute-done.44 = bf16[2,2,64,1024]{3,2,0,1:T(8,128)(2,1)S(1)} collective-permute-done((bf16[2,2,64,1024]{3,2,0,1:T(8,128)(2,1)S(1)}, bf16[2,2,64,1024]{3,2,0,1:T(8,128)(2,1)S(1)}, u32[]{:S(2)}, u32[]{:S(2)}) %collective-permute-start.44) | collective-permute-done | bytes 524320 | tf_op jit(solution)/shard_map/ppermute | solution.py:70
  601.4 11.2 %collective-permute-done.39 = bf16[2,2,2,64,1152]{4,3,0,1,2:T(8,128)(2,1)S(1)} collective-permute-done((bf16[2,2,2,64,1152]{4,3,0,1,2:T(8,128)(2,1)S(1)}, bf16[2,2,2,64,1152]{4,3,0,1,2:T(8,128)(2,1)S(1)}, u32[]{:S(2)}, u32[]{:S(2)}) %collective-permute-start.39) | collective-permute-done | bytes 1179680 | tf_op jit(solution)/shard_map/ppermute | solution.py:70
  612.8 12.0 %collective-permute-done.36 = bf16[2,2,64,1152]{3,2,0,1:T(8,128)(2,1)S(1)} collective-permute-done((bf16[2,2,64,1152]{3,2,0,1:T(8,128)(2,1)S(1)}, bf16[2,2,64,1152]{3,2,0,1:T(8,128)(2,1)S(1)}, u32[]{:S(2)}, u32[]{:S(2)}) %collective-permute-start.36) | collective-permute-done | bytes 589856 | tf_op jit(solution)/shard_map/ppermute | solution.py:70
  629.5 4.8 collective-permute-done.46
  636.7 5.4 fusion.33
  652.9 5.8 fusion.30
  674.0 4.7 collective-permute-done.41
  681.2 5.1 collective-permute-done.42
  (802 shorter events, 340.4 us)
Async XLA Ops:
  2.4 17.6 %collective-permute-start = (bf16[64,1152]{1,0:T(8,128)(2,1)S(1)}, bf16[64,1152]{1,0:T(8,128)(2,1)S(1)}, u32[]{:S(2)}, u32[]{:S(2)}) collective-permute-start(bf16[64,1152]{1,0:T(8,128)(2,1)S(1)} %fusion.199), channel_id=1, source_target_pairs={{0,16},{2,18},{4,20},{6,22},{8,24},{10,26},{12,28},{14,30},{16,0},... | collective-permute-start | bytes 442376 | tf_op jit(solution)/shard_map/ppermute | solution.py:49
  7.5 12.5 %collective-permute-start.4 = (bf16[64,1152]{1,0:T(8,128)(2,1)S(1)}, bf16[64,1152]{1,0:T(8,128)(2,1)S(1)}, u32[]{:S(2)}, u32[]{:S(2)}) collective-permute-start(bf16[64,1152]{1,0:T(8,128)(2,1)S(1)} %concatenate.74), channel_id=1, source_target_pairs={{0,16},{2,18},{4,20},{6,22},{8,24},{10,26},{12,28},{14,30},{16,0},... | collective-permute-start | bytes 442376 | tf_op jit(solution)/shard_map/ppermute | solution.py:49
  22.8 12.2 %collective-permute-start.1 = (bf16[2,64,1152]{2,1,0:T(8,128)(2,1)S(1)}, bf16[2,64,1152]{2,1,0:T(8,128)(2,1)S(1)}, u32[]{:S(2)}, u32[]{:S(2)}) collective-permute-start(bf16[2,64,1152]{2,1,0:T(8,128)(2,1)S(1)} %pad_maximum_fusion.24), channel_id=1, source_target_pairs={{0,8},{2,10},{4,12},{6,14},{8,0},{10,2},{12,4},{14,6},{16,24},{18,... | collective-permute-start | bytes 884744 | tf_op jit(solution)/shard_map/ppermute | solution.py:49
  30.3 12.5 %collective-permute-start.6 = (bf16[2,2,64,1152]{3,2,0,1:T(8,128)(2,1)S(1)}, bf16[2,2,64,1152]{3,2,0,1:T(8,128)(2,1)S(1)}, u32[]{:S(2)}, u32[]{:S(2)}) collective-permute-start(bf16[2,2,64,1152]{3,2,0,1:T(8,128)(2,1)S(1)} %pad_maximum_fusion.16), channel_id=1, source_target_pairs={{0,2},{2,0},{4,6},{6,4},{8,10},{10,8},{12,14},{14,12},{16,18},{18,... | collective-permute-start | bytes 1769480 | tf_op jit(solution)/shard_map/ppermute | solution.py:49
  36.0 16.6 %collective-permute-start.2 = (bf16[2,2,64,1152]{3,2,1,0:T(8,128)(2,1)}, bf16[2,2,64,1152]{3,2,1,0:T(8,128)(2,1)}, u32[]{:S(2)}, u32[]{:S(2)}) collective-permute-start(bf16[2,2,64,1152]{3,2,1,0:T(8,128)(2,1)} %pad_maximum_fusion.15), channel_id=1, source_target_pairs={{0,4},{2,6},{4,0},{6,2},{8,12},{10,14},{12,8},{14,10},{16,20},{18,... | collective-permute-start | bytes 1769480 | tf_op jit(solution)/shard_map/ppermute | solution.py:49
  44.0 31.5 %collective-permute-start.7 = (bf16[2,2,2,64,1152]{4,3,0,1,2:T(8,128)(2,1)}, bf16[2,2,2,64,1152]{4,3,0,1,2:T(8,128)(2,1)}, u32[]{:S(2)}, u32[]{:S(2)}) collective-permute-start(bf16[2,2,2,64,1152]{4,3,0,1,2:T(8,128)(2,1)} %pad_maximum_fusion.10), channel_id=1, source_target_pairs={{0,4},{2,6},{4,0},{6,2},{8,12},{10,14},{12,8},{14,10},{16,20},{18,... | collective-permute-start | bytes 3538952 | tf_op jit(solution)/shard_map/ppermute | solution.py:49
  56.0 23.5 %collective-permute-start.3 = (bf16[2,2,2,64,1152]{4,3,2,1,0:T(8,128)(2,1)}, bf16[2,2,2,64,1152]{4,3,2,1,0:T(8,128)(2,1)}, u32[]{:S(2)}, u32[]{:S(2)}) collective-permute-start(bf16[2,2,2,64,1152]{4,3,2,1,0:T(8,128)(2,1)} %pad_maximum_fusion.9), channel_id=1, source_target_pairs={{0,2},{2,0},{4,6},{6,4},{8,10},{10,8},{12,14},{14,12},{16,18},{18,... | collective-permute-start | bytes 3538952 | tf_op jit(solution)/shard_map/ppermute | solution.py:49
  111.0 66.7 %collective-permute-start.14 = (bf16[64,1024]{1,0:T(8,128)(2,1)}, bf16[64,1024]{1,0:T(8,128)(2,1)}, u32[]{:S(2)}, u32[]{:S(2)}) collective-permute-start(bf16[64,1024]{1,0:T(8,128)(2,1)} %param.46), channel_id=1, source_target_pairs={{0,16},{2,18},{4,20},{6,22},{8,24},{10,26},{12,28},{14,30},{16,0},... | collective-permute-start | bytes 393224 | tf_op jit(solution)/shard_map/ppermute | solution.py:49
  113.1 67.3 %collective-permute-start.18 = (bf16[64,1024]{1,0:T(8,128)(2,1)}, bf16[64,1024]{1,0:T(8,128)(2,1)}, u32[]{:S(2)}, u32[]{:S(2)}) collective-permute-start(bf16[64,1024]{1,0:T(8,128)(2,1)} %param.47), channel_id=1, source_target_pairs={{0,16},{2,18},{4,20},{6,22},{8,24},{10,26},{12,28},{14,30},{16,0},... | collective-permute-start | bytes 393224 | tf_op jit(solution)/shard_map/ppermute | solution.py:49
  163.1 11.7 %collective-permute-start.8 = (f32[1024,1]{0,1:T(1,128)S(1)}, f32[1024,1]{0,1:T(1,128)S(1)}, u32[]{:S(2)}, u32[]{:S(2)}) collective-permute-start(f32[1024,1]{0,1:T(1,128)S(1)} %bitcast.776), channel_id=1, source_target_pairs={{0,1},{1,0},{2,3},{3,2},{4,5},{5,4},{6,7},{7,6},{8,9},{9,8},{10,11... | collective-permute-start | bytes 12296 | tf_op jit(solution)/shard_map/ppermute | solution.py:22
  171.8 12.9 %collective-permute-start.9 = (bf16[64,1024]{1,0:T(8,128)(2,1)S(1)}, bf16[64,1024]{1,0:T(8,128)(2,1)S(1)}, u32[]{:S(2)}, u32[]{:S(2)}) collective-permute-start(bf16[64,1024]{1,0:T(8,128)(2,1)S(1)} %copy-done.88), channel_id=1, source_target_pairs={{0,16},{2,18},{4,20},{6,22},{8,24},{10,26},{12,28},{14,30},{16,0},... | collective-permute-start | bytes 393224 | tf_op jit(solution)/shard_map/ppermute | solution.py:49
  174.0 13.2 %collective-permute-start.22 = (bf16[64,1024]{1,0:T(8,128)(2,1)}, bf16[64,1024]{1,0:T(8,128)(2,1)S(1)}, u32[]{:S(2)}, u32[]{:S(2)}) collective-permute-start(bf16[64,1024]{1,0:T(8,128)(2,1)} %bitcast.3), channel_id=1, source_target_pairs={{0,16},{2,18},{4,20},{6,22},{8,24},{10,26},{12,28},{14,30},{16,0},... | collective-permute-start | bytes 393224 | tf_op jit(solution)/shard_map/ppermute | solution.py:49
  179.0 13.7 %collective-permute-start.15 = (bf16[2,64,1024]{2,1,0:T(8,128)(2,1)S(1)}, bf16[2,64,1024]{2,1,0:T(8,128)(2,1)S(1)}, u32[]{:S(2)}, u32[]{:S(2)}) collective-permute-start(bf16[2,64,1024]{2,1,0:T(8,128)(2,1)S(1)} %pad_maximum_fusion.28), channel_id=1, source_target_pairs={{0,8},{2,10},{4,12},{6,14},{8,0},{10,2},{12,4},{14,6},{16,24},{18,... | collective-permute-start | bytes 786440 | tf_op jit(solution)/shard_map/ppermute | solution.py:49
  181.4 23.1 %collective-permute-start.19 = (bf16[2,64,1024]{2,1,0:T(8,128)(2,1)S(1)}, bf16[2,64,1024]{2,1,0:T(8,128)(2,1)S(1)}, u32[]{:S(2)}, u32[]{:S(2)}) collective-permute-start(bf16[2,64,1024]{2,1,0:T(8,128)(2,1)S(1)} %pad_maximum_fusion.29), channel_id=1, source_target_pairs={{0,8},{2,10},{4,12},{6,14},{8,0},{10,2},{12,4},{14,6},{16,24},{18,... | collective-permute-start | bytes 786440 | tf_op jit(solution)/shard_map/ppermute | solution.py:49
  184.8 19.2 %collective-permute-start.10 = (bf16[2,64,1024]{2,1,0:T(8,128)(2,1)S(1)}, bf16[2,64,1024]{2,1,0:T(8,128)(2,1)S(1)}, u32[]{:S(2)}, u32[]{:S(2)}) collective-permute-start(bf16[2,64,1024]{2,1,0:T(8,128)(2,1)S(1)} %pad_maximum_fusion.27), channel_id=1, source_target_pairs={{0,8},{2,10},{4,12},{6,14},{8,0},{10,2},{12,4},{14,6},{16,24},{18,... | collective-permute-start | bytes 786440 | tf_op jit(solution)/shard_map/ppermute | solution.py:49
  188.1 20.5 %collective-permute-start.23 = (bf16[2,64,1024]{2,1,0:T(8,128)(2,1)S(1)}, bf16[2,64,1024]{2,1,0:T(8,128)(2,1)S(1)}, u32[]{:S(2)}, u32[]{:S(2)}) collective-permute-start(bf16[2,64,1024]{2,1,0:T(8,128)(2,1)S(1)} %pad_maximum_fusion.30), channel_id=1, source_target_pairs={{0,8},{2,10},{4,12},{6,14},{8,0},{10,2},{12,4},{14,6},{16,24},{18,... | collective-permute-start | bytes 786440 | tf_op jit(solution)/shard_map/ppermute | solution.py:49
  192.8 24.8 %collective-permute-start.16 = (bf16[2,2,64,1024]{3,2,1,0:T(8,128)(2,1)S(1)}, bf16[2,2,64,1024]{3,2,1,0:T(8,128)(2,1)S(1)}, u32[]{:S(2)}, u32[]{:S(2)}) collective-permute-start(bf16[2,2,64,1024]{3,2,1,0:T(8,128)(2,1)S(1)} %pad_maximum_fusion.20), channel_id=1, source_target_pairs={{0,4},{2,6},{4,0},{6,2},{8,12},{10,14},{12,8},{14,10},{16,20},{18,... | collective-permute-start | bytes 1572872 | tf_op jit(solution)/shard_map/ppermute | solution.py:49
  204.1 12.0 %collective-permute-start.11 = (bf16[2,2,64,1024]{3,2,1,0:T(8,128)(2,1)S(1)}, bf16[2,2,64,1024]{3,2,1,0:T(8,128)(2,1)S(1)}, u32[]{:S(2)}, u32[]{:S(2)}) collective-permute-start(bf16[2,2,64,1024]{3,2,1,0:T(8,128)(2,1)S(1)} %pad_maximum_fusion.19), channel_id=1, source_target_pairs={{0,4},{2,6},{4,0},{6,2},{8,12},{10,14},{12,8},{14,10},{16,20},{18,... | collective-permute-start | bytes 1572872 | tf_op jit(solution)/shard_map/ppermute | solution.py:49
  204.7 14.9 %collective-permute-start.20 = (bf16[2,2,64,1024]{3,2,0,1:T(8,128)(2,1)S(1)}, bf16[2,2,64,1024]{3,2,0,1:T(8,128)(2,1)S(1)}, u32[]{:S(2)}, u32[]{:S(2)}) collective-permute-start(bf16[2,2,64,1024]{3,2,0,1:T(8,128)(2,1)S(1)} %pad_maximum_fusion.21), channel_id=1, source_target_pairs={{0,2},{2,0},{4,6},{6,4},{8,10},{10,8},{12,14},{14,12},{16,18},{18,... | collective-permute-start | bytes 1572872 | tf_op jit(solution)/shard_map/ppermute | solution.py:49
  208.7 22.2 %collective-permute-start.24 = (bf16[2,2,64,1024]{3,2,0,1:T(8,128)(2,1)S(1)}, bf16[2,2,64,1024]{3,2,0,1:T(8,128)(2,1)S(1)}, u32[]{:S(2)}, u32[]{:S(2)}) collective-permute-start(bf16[2,2,64,1024]{3,2,0,1:T(8,128)(2,1)S(1)} %pad_maximum_fusion.22), channel_id=1, source_target_pairs={{0,2},{2,0},{4,6},{6,4},{8,10},{10,8},{12,14},{14,12},{16,18},{18,... | collective-permute-start | bytes 1572872 | tf_op jit(solution)/shard_map/ppermute | solution.py:49
  216.3 37.1 %collective-permute-start.12 = (bf16[2,2,2,64,1024]{4,3,2,1,0:T(8,128)(2,1)S(1)}, bf16[2,2,2,64,1024]{4,3,2,1,0:T(8,128)(2,1)S(1)}, u32[]{:S(2)}, u32[]{:S(2)}) collective-permute-start(bf16[2,2,2,64,1024]{4,3,2,1,0:T(8,128)(2,1)S(1)} %pad_maximum_fusion.11), channel_id=1, source_target_pairs={{0,2},{2,0},{4,6},{6,4},{8,10},{10,8},{12,14},{14,12},{16,18},{18,... | collective-permute-start | bytes 3145736 | tf_op jit(solution)/shard_map/ppermute | solution.py:49
  218.9 54.7 %collective-permute-start.17 = (bf16[2,2,2,64,1024]{4,3,2,1,0:T(8,128)(2,1)}, bf16[2,2,2,64,1024]{4,3,2,1,0:T(8,128)(2,1)}, u32[]{:S(2)}, u32[]{:S(2)}) collective-permute-start(bf16[2,2,2,64,1024]{4,3,2,1,0:T(8,128)(2,1)} %pad_maximum_fusion.12), channel_id=1, source_target_pairs={{0,2},{2,0},{4,6},{6,4},{8,10},{10,8},{12,14},{14,12},{16,18},{18,... | collective-permute-start | bytes 3145736 | tf_op jit(solution)/shard_map/ppermute | solution.py:49
  220.9 54.8 %collective-permute-start.21 = (bf16[2,2,2,64,1024]{4,3,0,1,2:T(8,128)(2,1)}, bf16[2,2,2,64,1024]{4,3,0,1,2:T(8,128)(2,1)}, u32[]{:S(2)}, u32[]{:S(2)}) collective-permute-start(bf16[2,2,2,64,1024]{4,3,0,1,2:T(8,128)(2,1)} %pad_maximum_fusion.13), channel_id=1, source_target_pairs={{0,4},{2,6},{4,0},{6,2},{8,12},{10,14},{12,8},{14,10},{16,20},{18,... | collective-permute-start | bytes 3145736 | tf_op jit(solution)/shard_map/ppermute | solution.py:49
  232.1 46.4 %collective-permute-start.25 = (bf16[2,2,2,64,1024]{4,3,0,1,2:T(8,128)(2,1)}, bf16[2,2,2,64,1024]{4,3,0,1,2:T(8,128)(2,1)}, u32[]{:S(2)}, u32[]{:S(2)}) collective-permute-start(bf16[2,2,2,64,1024]{4,3,0,1,2:T(8,128)(2,1)} %pad_maximum_fusion.14), channel_id=1, source_target_pairs={{0,4},{2,6},{4,0},{6,2},{8,12},{10,14},{12,8},{14,10},{16,20},{18,... | collective-permute-start | bytes 3145736 | tf_op jit(solution)/shard_map/ppermute | solution.py:49
  259.6 26.4 %collective-permute-start.13 = (bf16[1024,1024]{0,1:T(8,128)(2,1)}, bf16[1024,1024]{0,1:T(8,128)(2,1)}, u32[]{:S(2)}, u32[]{:S(2)}) collective-permute-start(bf16[1024,1024]{0,1:T(8,128)(2,1)} %get-tuple-element.343), channel_id=1, source_target_pairs={{0,1},{1,0},{2,3},{3,2},{4,5},{5,4},{6,7},{7,6},{8,9},{9,8},{10,11... | collective-permute-start | bytes 6291464 | tf_op jit(solution)/shard_map/ppermute | solution.py:22
  303.8 26.2 %collective-permute-start.55 = (bf16[2,2,2,64,1024]{4,3,0,1,2:T(8,128)(2,1)S(1)}, bf16[2,2,2,64,1024]{4,3,0,1,2:T(8,128)(2,1)S(1)}, u32[]{:S(2)}, u32[]{:S(2)}) collective-permute-start(bf16[2,2,2,64,1024]{4,3,0,1,2:T(8,128)(2,1)S(1)} %fusion.161), channel_id=1, source_target_pairs={{0,4},{2,6},{4,0},{6,2},{8,12},{10,14},{12,8},{14,10},{16,20},{18,... | collective-permute-start | bytes 3145736 | tf_op jit(solution)/shard_map/ppermute | solution.py:70
  307.1 42.1 %collective-permute-start.51 = (bf16[2,2,2,64,1024]{4,3,0,1,2:T(8,128)(2,1)S(1)}, bf16[2,2,2,64,1024]{4,3,0,1,2:T(8,128)(2,1)S(1)}, u32[]{:S(2)}, u32[]{:S(2)}) collective-permute-start(bf16[2,2,2,64,1024]{4,3,0,1,2:T(8,128)(2,1)S(1)} %fusion.160), channel_id=1, source_target_pairs={{0,4},{2,6},{4,0},{6,2},{8,12},{10,14},{12,8},{14,10},{16,20},{18,... | collective-permute-start | bytes 3145736 | tf_op jit(solution)/shard_map/ppermute | solution.py:70
  311.0 40.4 %collective-permute-start.47 = (bf16[2,2,2,64,1024]{4,3,0,1,2:T(8,128)(2,1)S(1)}, bf16[2,2,2,64,1024]{4,3,0,1,2:T(8,128)(2,1)S(1)}, u32[]{:S(2)}, u32[]{:S(2)}) collective-permute-start(bf16[2,2,2,64,1024]{4,3,0,1,2:T(8,128)(2,1)S(1)} %fusion.159), channel_id=1, source_target_pairs={{0,2},{2,0},{4,6},{6,4},{8,10},{10,8},{12,14},{14,12},{16,18},{18,... | collective-permute-start | bytes 3145736 | tf_op jit(solution)/shard_map/ppermute | solution.py:70
  312.6 78.3 %collective-permute-start.26 = (bf16[1024,1024]{0,1:T(8,128)(2,1)}, bf16[1024,1024]{0,1:T(8,128)(2,1)}, u32[]{:S(2)}, u32[]{:S(2)}) collective-permute-start(bf16[1024,1024]{0,1:T(8,128)(2,1)} %get-tuple-element.347), channel_id=1, source_target_pairs={{0,1},{1,0},{2,3},{3,2},{4,5},{5,4},{6,7},{7,6},{8,9},{9,8},{10,11... | collective-permute-start | bytes 6291464 | tf_op jit(solution)/shard_map/ppermute | solution.py:22
  322.7 66.1 %collective-permute-start.27 = (bf16[1024,1024]{0,1:T(8,128)(2,1)S(1)}, bf16[1024,1024]{0,1:T(8,128)(2,1)S(1)}, u32[]{:S(2)}, u32[]{:S(2)}) collective-permute-start(bf16[1024,1024]{0,1:T(8,128)(2,1)S(1)} %get-tuple-element.345), channel_id=1, source_target_pairs={{0,1},{1,0},{2,3},{3,2},{4,5},{5,4},{6,7},{7,6},{8,9},{9,8},{10,11... | collective-permute-start | bytes 6291464 | tf_op jit(solution)/shard_map/ppermute | solution.py:22
  330.4 21.9 %collective-permute-start.56 = (bf16[2,2,64,1024]{3,2,0,1:T(8,128)(2,1)S(1)}, bf16[2,2,64,1024]{3,2,0,1:T(8,128)(2,1)S(1)}, u32[]{:S(2)}, u32[]{:S(2)}) collective-permute-start(bf16[2,2,64,1024]{3,2,0,1:T(8,128)(2,1)S(1)} %fusion.173), channel_id=1, source_target_pairs={{0,2},{2,0},{4,6},{6,4},{8,10},{10,8},{12,14},{14,12},{16,18},{18,... | collective-permute-start | bytes 1572872 | tf_op jit(solution)/shard_map/ppermute | solution.py:70
  349.8 10.8 %collective-permute-start.52 = (bf16[2,2,64,1024]{3,2,0,1:T(8,128)(2,1)S(1)}, bf16[2,2,64,1024]{3,2,0,1:T(8,128)(2,1)S(1)}, u32[]{:S(2)}, u32[]{:S(2)}) collective-permute-start(bf16[2,2,64,1024]{3,2,0,1:T(8,128)(2,1)S(1)} %fusion.172), channel_id=1, source_target_pairs={{0,2},{2,0},{4,6},{6,4},{8,10},{10,8},{12,14},{14,12},{16,18},{18,... | collective-permute-start | bytes 1572872 | tf_op jit(solution)/shard_map/ppermute | solution.py:70
  362.5 15.7 %collective-permute-start.49 = (bf16[2,64,1024]{2,1,0:T(8,128)(2,1)S(1)}, bf16[2,64,1024]{2,1,0:T(8,128)(2,1)S(1)}, u32[]{:S(2)}, u32[]{:S(2)}) collective-permute-start(bf16[2,64,1024]{2,1,0:T(8,128)(2,1)S(1)} %fusion.189), channel_id=1, source_target_pairs={{0,8},{2,10},{4,12},{6,14},{8,0},{10,2},{12,4},{14,6},{16,24},{18,... | collective-permute-start | bytes 786440 | tf_op jit(solution)/shard_map/ppermute | solution.py:70
  363.3 17.8 %collective-permute-start.58 = (bf16[64,1024]{1,0:T(8,128)(2,1)S(1)}, bf16[64,1024]{1,0:T(8,128)(2,1)S(1)}, u32[]{:S(2)}, u32[]{:S(2)}) collective-permute-start(bf16[64,1024]{1,0:T(8,128)(2,1)S(1)} %fusion.205), channel_id=1, source_target_pairs={{0,16},{2,18},{4,20},{6,22},{8,24},{10,26},{12,28},{14,30},{16,0},... | collective-permute-start | bytes 393224 | tf_op jit(solution)/shard_map/ppermute | solution.py:70
  370.3 16.3 %collective-permute-start.54 = (bf16[64,1024]{1,0:T(8,128)(2,1)S(1)}, bf16[64,1024]{1,0:T(8,128)(2,1)S(1)}, u32[]{:S(2)}, u32[]{:S(2)}) collective-permute-start(bf16[64,1024]{1,0:T(8,128)(2,1)S(1)} %fusion.204), channel_id=1, source_target_pairs={{0,16},{2,18},{4,20},{6,22},{8,24},{10,26},{12,28},{14,30},{16,0},... | collective-permute-start | bytes 393224 | tf_op jit(solution)/shard_map/ppermute | solution.py:70
  423.4 161.0 %collective-permute-start.43 = (bf16[2,2,2,64,1024]{4,3,0,1,2:T(8,128)(2,1)}, bf16[2,2,2,64,1024]{4,3,0,1,2:T(8,128)(2,1)}, u32[]{:S(2)}, u32[]{:S(2)}) collective-permute-start(bf16[2,2,2,64,1024]{4,3,0,1,2:T(8,128)(2,1)} %fusion.158), channel_id=1, source_target_pairs={{0,2},{2,0},{4,6},{6,4},{8,10},{10,8},{12,14},{14,12},{16,18},{18,... | collective-permute-start | bytes 3145736 | tf_op jit(solution)/shard_map/ppermute | solution.py:70
  426.3 26.1 %collective-permute-start.28 = (f32[1024,1]{0,1:T(1,128)}, f32[1024,1]{0,1:T(1,128)}, u32[]{:S(2)}, u32[]{:S(2)}) collective-permute-start(f32[1024,1]{0,1:T(1,128)} %bitcast.120), channel_id=1, source_target_pairs={{0,1},{1,0},{2,3},{3,2},{4,5},{5,4},{6,7},{7,6},{8,9},{9,8},{10,11... | collective-permute-start | bytes 12296 | tf_op jit(solution)/shard_map/ppermute | solution.py:22
  558.5 15.8 %collective-permute-start.30 = (bf16[1024,256]{1,0:T(8,128)(2,1)}, bf16[1024,256]{1,0:T(8,128)(2,1)}, u32[]{:S(2)}, u32[]{:S(2)}) collective-permute-start(bf16[1024,256]{1,0:T(8,128)(2,1)} %fusion.167), channel_id=1, source_target_pairs={{0,1},{1,0},{2,3},{3,2},{4,5},{5,4},{6,7},{7,6},{8,9},{9,8},{10,11... | collective-permute-start | bytes 1572872 | tf_op jit(solution)/shard_map/ppermute | solution.py:22
  561.8 29.2 %collective-permute-start.35 = (bf16[2,2,2,64,1152]{4,3,0,1,2:T(8,128)(2,1)}, bf16[2,2,2,64,1152]{4,3,0,1,2:T(8,128)(2,1)}, u32[]{:S(2)}, u32[]{:S(2)}) collective-permute-start(bf16[2,2,2,64,1152]{4,3,0,1,2:T(8,128)(2,1)} %fusion.123), channel_id=1, source_target_pairs={{0,4},{2,6},{4,0},{6,2},{8,12},{10,14},{12,8},{14,10},{16,20},{18,... | collective-permute-start | bytes 3538952 | tf_op jit(solution)/shard_map/ppermute | solution.py:70
  573.0 63.6 %collective-permute-start.29 = (bf16[1024,1024]{0,1:T(8,128)(2,1)}, bf16[1024,1024]{0,1:T(8,128)(2,1)}, u32[]{:S(2)}, u32[]{:S(2)}) collective-permute-start(bf16[1024,1024]{0,1:T(8,128)(2,1)} %get-tuple-element.357), channel_id=1, source_target_pairs={{0,1},{1,0},{2,3},{3,2},{4,5},{5,4},{6,7},{7,6},{8,9},{9,8},{10,11... | collective-permute-start | bytes 6291464 | tf_op jit(solution)/shard_map/ppermute | solution.py:22
  583.8 28.8 %collective-permute-start.39 = (bf16[2,2,2,64,1152]{4,3,0,1,2:T(8,128)(2,1)S(1)}, bf16[2,2,2,64,1152]{4,3,0,1,2:T(8,128)(2,1)S(1)}, u32[]{:S(2)}, u32[]{:S(2)}) collective-permute-start(bf16[2,2,2,64,1152]{4,3,0,1,2:T(8,128)(2,1)S(1)} %fusion.124), channel_id=1, source_target_pairs={{0,2},{2,0},{4,6},{6,4},{8,10},{10,8},{12,14},{14,12},{16,18},{18,... | collective-permute-start | bytes 3538952 | tf_op jit(solution)/shard_map/ppermute | solution.py:70
  586.0 15.1 %collective-permute-start.44 = (bf16[2,2,64,1024]{3,2,0,1:T(8,128)(2,1)S(1)}, bf16[2,2,64,1024]{3,2,0,1:T(8,128)(2,1)S(1)}, u32[]{:S(2)}, u32[]{:S(2)}) collective-permute-start(bf16[2,2,64,1024]{3,2,0,1:T(8,128)(2,1)S(1)} %fusion.170), channel_id=1, source_target_pairs={{0,4},{2,6},{4,0},{6,2},{8,12},{10,14},{12,8},{14,10},{16,20},{18,... | collective-permute-start | bytes 1572872 | tf_op jit(solution)/shard_map/ppermute | solution.py:70
  592.5 32.3 %collective-permute-start.36 = (bf16[2,2,64,1152]{3,2,0,1:T(8,128)(2,1)S(1)}, bf16[2,2,64,1152]{3,2,0,1:T(8,128)(2,1)S(1)}, u32[]{:S(2)}, u32[]{:S(2)}) collective-permute-start(bf16[2,2,64,1152]{3,2,0,1:T(8,128)(2,1)S(1)} %fusion.168), channel_id=1, source_target_pairs={{0,2},{2,0},{4,6},{6,4},{8,10},{10,8},{12,14},{14,12},{16,18},{18,... | collective-permute-start | bytes 1769480 | tf_op jit(solution)/shard_map/ppermute | solution.py:70
  601.3 23.8 %collective-permute-start.45 = (bf16[2,64,1024]{2,1,0:T(8,128)(2,1)S(1)}, bf16[2,64,1024]{2,1,0:T(8,128)(2,1)S(1)}, u32[]{:S(2)}, u32[]{:S(2)}) collective-permute-start(bf16[2,64,1024]{2,1,0:T(8,128)(2,1)S(1)} %fusion.188), channel_id=1, source_target_pairs={{0,8},{2,10},{4,12},{6,14},{8,0},{10,2},{12,4},{14,6},{16,24},{18,... | collective-permute-start | bytes 786440 | tf_op jit(solution)/shard_map/ppermute | solution.py:70
  625.0 11.5 %collective-permute-start.37 = (bf16[2,64,1152]{2,1,0:T(8,128)(2,1)S(1)}, bf16[2,64,1152]{2,1,0:T(8,128)(2,1)S(1)}, u32[]{:S(2)}, u32[]{:S(2)}) collective-permute-start(bf16[2,64,1152]{2,1,0:T(8,128)(2,1)S(1)} %fusion.184), channel_id=1, source_target_pairs={{0,8},{2,10},{4,12},{6,14},{8,0},{10,2},{12,4},{14,6},{16,24},{18,... | collective-permute-start | bytes 884744 | tf_op jit(solution)/shard_map/ppermute | solution.py:70
  627.9 41.1 %collective-permute-start.40 = (bf16[2,2,64,1152]{3,2,0,1:T(8,128)(2,1)S(1)}, bf16[2,2,64,1152]{3,2,0,1:T(8,128)(2,1)}, u32[]{:S(2)}, u32[]{:S(2)}) collective-permute-start(bf16[2,2,64,1152]{3,2,0,1:T(8,128)(2,1)S(1)} %fusion.169), channel_id=1, source_target_pairs={{0,4},{2,6},{4,0},{6,2},{8,12},{10,14},{12,8},{14,10},{16,20},{18,... | collective-permute-start | bytes 1769480 | tf_op jit(solution)/shard_map/ppermute | solution.py:70
  643.5 20.9 %collective-permute-start.38 = (bf16[64,1152]{1,0:T(8,128)(2,1)}, bf16[64,1152]{1,0:T(8,128)(2,1)}, u32[]{:S(2)}, u32[]{:S(2)}) collective-permute-start(bf16[64,1152]{1,0:T(8,128)(2,1)} %fusion.200), channel_id=1, source_target_pairs={{0,16},{2,18},{4,20},{6,22},{8,24},{10,26},{12,28},{14,30},{16,0},... | collective-permute-start | bytes 442376 | tf_op jit(solution)/shard_map/ppermute | solution.py:70
  650.7 12.1 %collective-permute-start.33 = (f32[64,128]{1,0:T(8,128)}, f32[64,128]{1,0:T(8,128)}, u32[]{:S(2)}, u32[]{:S(2)}) collective-permute-start(f32[64,128]{1,0:T(8,128)} %fusion.345), channel_id=1, source_target_pairs={{0,8},{2,10},{4,12},{6,14},{8,0},{10,2},{12,4},{14,6},{16,24},{18,... | collective-permute-start | bytes 98312 | tf_op jit(solution)/shard_map/ppermute | solution.py:79
  (222 other events, 2123.6 us)
